TPU v7x, 32 devices: a whole 2x2x4 slice. The times are simulated.
32 devices in a mesh: row: 8 (over y, x, core), col: 4 (over z).
Axes of the slice: x: 2, y: 2, z: 4, core: 2. Of those that a mesh axis runs over, the one named last changes fastest.
Arguments:
- covariance: bfloat16 [16384, 16384], P('row', 'col'), as said below
- coef_index: int32 [3, 16384], replicated, may hold values from 0 to 127, as said below
Outputs:
- grid_cov: float32 [4608, 4608], P('row', 'col')
Inputs may be any that keep to these rules, and one draw needn't show every extreme that they name: `coef_index`: every (degree l, order m, parity c) with m <= l < 128, c in 0 and 1, and c = 0 where m = 0, names exactly one row. The rows of each order are consecutive: cosine terms by rising degree, then sine terms by rising degree. Orders m and 128 - m (0 and 64) stand next to each other, the smaller first, and fill 2 * 128 rows together; pairs start at multiples of 256. Columns follow the same index. `covariance`: Symmetric.
All inputs are finite; a program needn't handle non-finite values.
Results may differ from a plain program's by a relative error of at most 0.0028.
Values sent between devices are 32-bit elements; how exact they have to be, the bound alone decides.
No kernel may reach another device: no remote copies, remote signals or barrier semaphores. Data moves between devices by JAX's collectives and lax.ppermute only.
A program may use at most 128 MiB of HBM per device.

v0:
```python
import math

import jax
import jax.numpy as jnp
from jax import lax
from jax.sharding import PartitionSpec as P

LL = 128
NLON = 384
NLAT = 12


def legendre_rows(lat_count, lon_count, degree_count):
    grid_rows = lon_count // 2
    first_row = grid_rows // 2 - lat_count // 2
    colatitude = (first_row + jnp.arange(lat_count, dtype=jnp.float32) + 0.5) * (
        math.pi / grid_rows
    )
    cosine = jnp.cos(colatitude)[:, None]
    sine_vals = jnp.sin(colatitude)[:, None]
    orders = jnp.arange(degree_count, dtype=jnp.float32)[None, :]
    growth = jnp.sqrt((2.0 * orders + 1.0) / jnp.maximum(2.0 * orders, 1.0))
    growth = jnp.where(
        orders == 1.0, jnp.sqrt(jnp.float32(3.0)), jnp.where(orders == 0.0, 1.0, growth)
    )
    sectoral = jnp.exp(jnp.cumsum(jnp.log(growth), axis=1) + orders * jnp.log(sine_vals))

    def advance(state_pair, degree):
        before, earlier = state_pair
        deg_sum = degree + orders
        deg_diff = degree - orders
        alpha_lm = jnp.sqrt(
            jnp.maximum((2.0 * degree - 1.0) * (2.0 * degree + 1.0), 0.0)
            / jnp.maximum(deg_diff * deg_sum, 1.0)
        )
        beta_lm = jnp.sqrt(
            jnp.maximum((2.0 * degree + 1.0) * (deg_sum - 1.0) * (deg_diff - 1.0), 0.0)
            / jnp.maximum(deg_diff * deg_sum * (2.0 * degree - 3.0), 1.0)
        )
        general = alpha_lm * cosine * before - beta_lm * earlier
        current = jnp.where(orders < degree, general, jnp.where(orders == degree, sectoral, 0.0))
        return ((current, before), current)

    start_pair = (
        jnp.zeros((lat_count, degree_count), jnp.float32),
        jnp.zeros((lat_count, degree_count), jnp.float32),
    )
    _, stacked = lax.scan(
        advance, start_pair, jnp.arange(degree_count, dtype=jnp.float32), unroll=16
    )
    return jnp.transpose(stacked, (1, 0, 2)).reshape(lat_count, degree_count * degree_count)


def fourier(modes, parity, longitudes):
    phases = longitudes[:, None] * modes[None, :] % NLON
    angles = phases.astype(jnp.float32) * (2.0 * math.pi / NLON)
    return jnp.where(parity[None, :] == 0, jnp.cos(angles), jnp.sin(angles))


def block_slots(orders_flat, blocks, length, slot_count):
    grouped = orders_flat.reshape(blocks, length)
    change = jnp.concatenate(
        [jnp.ones((blocks, 1), jnp.int32), (grouped[:, 1:] != grouped[:, :-1]).astype(jnp.int32)],
        axis=1,
    )
    slot_ids = jnp.cumsum(change, axis=1) - 1
    first_marks = (
        slot_ids[:, :, None] == jnp.arange(slot_count, dtype=jnp.int32)[None, None, :]
    ) & (change[:, :, None] == 1)
    firsts = jnp.sum(jnp.where(first_marks, grouped[:, :, None], 0), axis=1)
    return (slot_ids, firsts)


def spectral_weights(plm_table, degree, orders, parity, slot_ids, slot_count):
    values = plm_table[:, degree * LL + orders]
    key_ids = 2 * slot_ids + parity
    matches = key_ids[None, None, :] == jnp.arange(2 * slot_count, dtype=jnp.int32)[None, :, None]
    return jnp.where(matches, values[:, None, :], 0.0)


def on_device(covariance, coef_index):
    rows_dev, cols_dev = covariance.shape
    row_count = lax.axis_size("row")
    col_count = lax.axis_size("col")
    row_place = lax.axis_index("row")
    col_place = lax.axis_index("col")
    row_orders = max(LL // row_count, 2)
    col_orders = max(LL // col_count, 2)
    plm_table = legendre_rows(NLAT, NLON, LL)
    row_slots, row_firsts = block_slots(coef_index[1], row_count, rows_dev, row_orders)
    col_slots, col_firsts = block_slots(coef_index[1], col_count, cols_dev, col_orders)
    mine_rows = lax.dynamic_slice_in_dim(coef_index, row_place * rows_dev, rows_dev, 1)
    mine_cols = lax.dynamic_slice_in_dim(coef_index, col_place * cols_dev, cols_dev, 1)
    own_row_slots = lax.dynamic_index_in_dim(row_slots, row_place, 0, keepdims=False)
    own_col_slots = lax.dynamic_index_in_dim(col_slots, col_place, 0, keepdims=False)
    row_weights = spectral_weights(
        plm_table, mine_rows[0], mine_rows[1], mine_rows[2], own_row_slots, row_orders
    )
    row_weights = row_weights.astype(jnp.bfloat16).reshape(NLAT * 2 * row_orders, rows_dev)
    col_weights = spectral_weights(
        plm_table, mine_cols[0], mine_cols[1], mine_cols[2], own_col_slots, col_orders
    )
    first_pass = jnp.dot(row_weights, covariance, preferred_element_type=jnp.float32)
    second = jnp.einsum("ak,jbk->ajb", first_pass, col_weights, precision=lax.Precision.HIGHEST)
    width_cols = NLAT * 2 * col_orders
    second = second.reshape(NLAT, 2 * row_orders, width_cols)
    all_lons = jnp.arange(NLON, dtype=jnp.int32)
    row_modes = jnp.repeat(row_firsts.reshape(-1), 2)
    row_parity = jnp.arange(row_modes.shape[0], dtype=jnp.int32) % 2
    row_table = fourier(row_modes, row_parity, all_lons)
    grid_vals = jnp.einsum(
        "jq,iqc->jic",
        row_table,
        lax.all_to_all(second, "row", split_axis=2, concat_axis=1, tiled=True),
        precision=lax.Precision.HIGHEST,
    )
    row_done = lax.all_to_all(grid_vals, "row", split_axis=0, concat_axis=2, tiled=True)
    pts_row = row_done.shape[0] * NLAT
    spectral = row_done.reshape(pts_row, NLAT, 2 * col_orders)
    own_modes = jnp.repeat(lax.dynamic_index_in_dim(col_firsts, col_place, 0, keepdims=False), 2)
    own_parity = jnp.arange(2 * col_orders, dtype=jnp.int32) % 2
    pts_col = NLAT * NLON // col_count
    longitudes = jnp.arange(pts_col * lax.axis_size("col") // NLAT, dtype=jnp.int32)
    table_part = fourier(own_modes, own_parity, longitudes)
    grid_vals = jnp.einsum("jk,pik->jip", table_part, spectral, precision=lax.Precision.HIGHEST)
    summed = lax.psum_scatter(
        grid_vals.reshape(pts_col * lax.axis_size("col"), pts_row),
        "col",
        scatter_dimension=0,
        tiled=True,
    )
    result = summed.T
    return result


def solution(mesh):
    in_specs = (P("row", "col"), P())
    out_specs = P("row", "col")
    return jax.shard_map(
        on_device, mesh=mesh, in_specs=in_specs, out_specs=out_specs, check_vma=False
    )
```

profile of v0, /device:TPU:0, one launch (start us, length us, event | category | flops | bytes accessed | tf_op | source)
XLA Modules:
  0.0 697.4 jit_solution(10786194116965163162)
XLA Ops:
  18.5 265.9 %while.19 = (s32[]{:T(128)}, f32[12,128]{1,0:T(8,128)S(1)}, f32[12,128]{1,0:T(8,128)S(1)}, f32[8,16,12,128]{3,2,1,0:T(8,128)S(1)}, f32[8,16]{1,0:T(8,128)S(1)}, ...) while((s32[]{:T(128)}, f32[12,128]{1,0:T(8,128)S(1)}, ...), condition=%wide.region_5.6_spmd.clone.clone, body=%wide.region_4.5_spmd.clone.clone.sunk | while | flops 359546 | bytes 878834 | solution.py:48
  284.4 4.7 copy.32
  289.1 9.0 %gather_fusion = bf16[2048,12]{1,0:T(8,128)(2,1)S(1)} fusion(f32[12,16384]{0,1:T(8,128)} %bitcast.387, s32[2048]{0:T(1024)S(1)} %broadcast_clamp_fusion.1), kind=kCustom, calls=%fused_computation | custom fusion | bytes 106496 | tf_op jit(solution)/shard_map/gather | solution.py:75
  298.1 14.1 %gather_fusion.1 = f32[4096,12]{1,0:T(8,128)S(1)} fusion(f32[12,16384]{0,1:T(8,128)} %bitcast.388, s32[4096]{0:T(1024)S(1)} %broadcast_clamp_fusion), kind=kCustom, calls=%fused_computation.1 | custom fusion | bytes 409600 | tf_op jit(solution)/shard_map/gather | solution.py:75
  313.4 10.3 %fusion.287 = f32[384,4096]{1,0:T(8,128)S(1)} fusion(bf16[384,2048]{1,0:T(8,128)(2,1)S(1)} %bitcast.395, bf16[2048,4096]{1,0:T(8,128)(2,1)} %param.4), kind=kOutput, calls=%fused_computation.418 | convolution fusion | flops 6442450944 | bytes 24641536 | tf_op jit(solution)/shard_map/dot_general | solution.py:103
  323.7 20.4 %fusion.215 = f32[384,12,64]{0,2,1:T(8,128)S(1)} fusion(f32[384,4096]{1,0:T(8,128)S(1)} %fusion.287, f32[12,4096]{1,0:T(8,128)S(1)} %copy.34, pred[64,4096]{1,0:T(8,128)(4,1)S(1)} %iota_compare_fusion.33), kind=kOutput, calls=%fused_computation.315 | convolution fusion | flops 14498660352 | bytes 7929856 | tf_op jit(solution)/shard_map/ak,jbk->ajb/dot_general | solution.py:104
  344.1 4.1 reshape.1758
  348.1 5.8 reshape.1775
  354.0 5.2 all-to-all-start
  359.9 16.1 %all-to-all-done = f32[8,1,36864]{2,1,0:T(1,128)S(1)} async-done(((f32[8,1,36864]{2,1,0:T(1,128)}), f32[8,1,36864]{2,1,0:T(1,128)S(1)}, u32[]{:S(2)}, u32[]{:S(2)}) %all-to-all-start) | async-done | bytes 1179680 | tf_op jit(solution)/shard_map/all_to_all | solution.py:114
  376.5 3.4 reduce.11
  379.9 4.8 reshape.1776
  384.7 4.6 copy.37
  389.8 3.6 fusion.226
  393.5 2.4 copy.39
  395.9 3.6 all-to-all-start.1
  400.8 36.6 %all-to-all-done.1 = f32[384,12,96]{2,1,0:T(8,128)S(1)} async-done(((f32[384,12,96]{2,1,0:T(8,128)}), f32[384,12,96]{2,1,0:T(8,128)S(1)}, u32[]{:S(2)}, u32[]{:S(2)}) %all-to-all-start.1) | async-done | bytes 1769504 | tf_op jit(solution)/shard_map/all_to_all | solution.py:117
  437.3 2.8 copy.41
  440.1 4.8 reshape.1624
  444.9 14.6 %convolution_bitcast_fusion = f32[384,12,576]{0,2,1:T(8,128)} fusion(f32[576,12,64]{2,1,0:T(8,128)} %reshape.1624, s32[64]{0:T(128)S(1)} %mul.2312, pred[64]{0:T(512)(128)(4,1)S(1)} %fusion.269), kind=kOutput, calls=%fused_computation.321 | convolution fusion | flops 2038677504 | bytes 12386624 | tf_op jit(solution)/shard_map/jk,pik->jip/dot_general | solution.py:125
  459.4 13.5 %copy.43 = f32[384,12,576]{2,1,0:T(8,128)} copy(f32[384,12,576]{0,2,1:T(8,128)} %convolution_bitcast_fusion) | data formatting | bytes 21233664 | tf_op jit(solution)/shard_map/jk,pik->jip/transpose | solution.py:125
  473.0 15.0 %reshape.1625 = f32[4608,576]{1,0:T(8,128)} reshape(f32[384,12,576]{2,1,0:T(8,128)} %copy.43) | data formatting | bytes 21233664 | tf_op jit(solution)/shard_map/reshape | solution.py:127
  488.0 198.7 %reduce-scatter.2.cloned.1.call-done = f32[1152,576]{1,0:T(8,128)} async-done(((f32[4608,576]{1,0:T(8,128)}), f32[1152,576]{1,0:T(8,128)}) %reduce-scatter.2.cloned.1.call-update) | async-done | bytes 2654224 | tf_op jit(solution)/shard_map/reduce_scatter | solution.py:126
  686.7 3.4 copy.44
  (472 shorter events, 198.8 us)
Async XLA Ops:
  289.1 24.0 %copy-start = (pred[32,2048]{1,0:T(8,128)(4,1)S(1)}, pred[32,2048]{1,0:T(8,128)(4,1)}, u32[]{:S(2)}) copy-start(pred[32,2048]{1,0:T(8,128)(4,1)} %iota_compare_fusion.35) | copy-start | bytes 196612
  348.1 11.0 %copy-start.1 = (pred[8,2048]{1,0:T(8,128)(4,1)S(1)}, pred[8,2048]{1,0:T(8,128)(4,1)}, u32[]{:S(2)}) copy-start(pred[8,2048]{1,0:T(8,128)(4,1)} %get-tuple-element.678) | copy-start | bytes 49156
  354.0 22.0 %all-to-all-start = ((f32[8,1,36864]{2,1,0:T(1,128)}), f32[8,1,36864]{2,1,0:T(1,128)S(1)}, u32[]{:S(2)}, u32[]{:S(2)}) async-start(f32[8,1,36864]{2,1,0:T(1,128)} %reshape.1775), calls=%async_computation | async-start | bytes 2359296 | tf_op jit(solution)/shard_map/all_to_all | solution.py:114
  395.9 41.5 %all-to-all-start.1 = ((f32[384,12,96]{2,1,0:T(8,128)}), f32[384,12,96]{2,1,0:T(8,128)S(1)}, u32[]{:S(2)}, u32[]{:S(2)}) async-start(f32[384,12,96]{2,1,0:T(8,128)} %copy.39), calls=%async_computation.1 | async-start | bytes 6291456 | tf_op jit(solution)/shard_map/all_to_all | solution.py:117
  399.5 287.2 %reduce-scatter.2.cloned.1.call-start = ((), (), s32[]{:S(2)}) async-start(), calls=%async_computation.3 | async-start | bytes 14745600 | tf_op jit(solution)/shard_map/reduce_scatter | solution.py:126
Sparse Core Ops, SparseCore 0:
  488.1 198.5 reduce-scatter.1
where the time goes:
time: 708 us; the launch traced here: 697 us
  waiting for transfers between devices  251 us (35%)
  other arithmetic  192 us (27%)
  local copies, waits for them, and re-layouts  99.1 us (14%)
  loops' own time  83 us (12%)
  matrix products  48.9 us (7%)
  between operations  14.1 us (2%)
  starting transfers between devices  9.12 us (1%)
    reduce_scatter x1, waiting for transfers between devices, on_device(): lax.psum_scatter(grid_vals.reshape(pts_col * lax.axis_size('col'), pts_ro...  199 us
    sqrt x128, other arithmetic, advance(): jnp.sqrt(jnp.maximum((2.0 * degree + 1.0) * (deg_sum - 1.0) * (deg_diff -...  83.6 us
    another operation x1, loops' own time, legendre_rows(): lax.scan(advance, start_pair, jnp.arange(degree_count, dtype=jnp.float32)...  83 us
    lt x128, other arithmetic, advance(): orders < degree  82 us
    all_to_all x1, waiting for transfers between devices, on_device(): lax.all_to_all(grid_vals, 'row', split_axis=0, concat_axis=2, tiled=True)  36.6 us
    gather x4, local copies, waits for them, and re-layouts, spectral_weights(): values = plm_table[:, degree * LL + orders]  24 us
    dot_general x1, matrix products, on_device(): jnp.einsum('ak,jbk->ajb', first_pass, col_weights, precision=lax.Precisio...  20.4 us
    all_to_all x1, waiting for transfers between devices, on_device(): lax.all_to_all(second, 'row', split_axis=2, concat_axis=1, tiled=True)  16.1 us
  transfers between devices with their start and end apart: 3, of which 3 were waited for; matrix products, arithmetic and copies ran while one was open for 0% of the time, Pallas kernels for 0%

commit v1 on v0

--- a/solution.py
+++ b/solution.py
@@ -1,13 +1,369 @@
+import functools
 import math
 
 import jax
 import jax.numpy as jnp
 from jax import lax
+from jax.experimental import pallas as pl
+from jax.experimental.pallas import tpu as pltpu
 from jax.sharding import PartitionSpec as P
 
 LL = 128
 NLON = 384
 NLAT = 12
+
+F32 = jnp.float32
+BF16 = jnp.bfloat16
+ROWS16 = 16
+CHIPS = 4
+CHUNKS = NLAT // CHIPS
+PAIR = 2 * LL
+KEYS = 4
+STEP = 2 * PAIR
+
+
+def split(x):
+    high = x.astype(BF16)
+    return high, (x - high.astype(F32)).astype(BF16)
+
+
+def dot3(a, b, dims):
+    dg = functools.partial(
+        lax.dot_general, dimension_numbers=(dims, ((), ())), preferred_element_type=F32
+    )
+    return dg(a[0], b[0]) + (dg(a[0], b[1]) + dg(a[1], b[0]))
+
+
+def turn4(xs):
+    lane = lax.broadcasted_iota(jnp.int32, xs[0].shape, 1)
+    left = lane < 64
+    even = (lane // 32) % 2 == 0
+    out = [None] * 4
+    halves = []
+    for u in range(2):
+        a, b = xs[u], xs[u + 2]
+        halves.append(
+            (jnp.where(left, a, pltpu.roll(b, 64, 1)), jnp.where(left, pltpu.roll(a, 64, 1), b))
+        )
+    for h in range(2):
+        a, b = halves[0][h], halves[1][h]
+        out[2 * h] = jnp.where(even, a, pltpu.roll(b, 32, 1))
+        out[2 * h + 1] = jnp.where(even, pltpu.roll(a, 96, 1), b)
+    return out
+
+
+def legendre_table(by_degree, by_order):
+    shape = (ROWS16, LL)
+    lat = lax.broadcasted_iota(jnp.int32, shape, 0).astype(F32)
+    colatitude = (NLON // 4 - NLAT // 2 + lat + 0.5) * (math.pi / (NLON // 2))
+    cosine, sine = jnp.cos(colatitude), jnp.sin(colatitude)
+    lane = lax.broadcasted_iota(jnp.int32, shape, 1)
+    orders = lane.astype(F32)
+    growth = jnp.sqrt((2.0 * orders + 1.0) / jnp.maximum(2.0 * orders, 1.0))
+    growth = jnp.where(lane == 1, math.sqrt(3.0), jnp.where(lane == 0, 1.0, growth))
+    total = jnp.log(growth)
+    shift = 1
+    while shift < LL:
+        total = total + jnp.where(lane >= shift, pltpu.roll(total, shift, 1), 0.0)
+        shift *= 2
+    sectoral = jnp.exp(total + orders * jnp.log(sine))
+    m8 = lax.broadcasted_iota(jnp.int32, (8, LL), 1).astype(F32)
+    r8 = lax.broadcasted_iota(jnp.int32, (8, LL), 0)
+
+    def block(b, carry):
+        before, earlier = carry
+        degree = (r8 + b * 8).astype(F32)
+        plus, minus = degree + m8, degree - m8
+        alpha = jnp.sqrt(
+            jnp.maximum((2.0 * degree - 1.0) * (2.0 * degree + 1.0), 0.0)
+            / jnp.maximum(minus * plus, 1.0)
+        )
+        beta = jnp.sqrt(
+            jnp.maximum((2.0 * degree + 1.0) * (plus - 1.0) * (minus - 1.0), 0.0)
+            / jnp.maximum(minus * plus * (2.0 * degree - 3.0), 1.0)
+        )
+        for r in range(8):
+            l = b * 8 + r
+            general = alpha[r : r + 1] * cosine * before - beta[r : r + 1] * earlier
+            current = jnp.where(lane < l, general, jnp.where(lane == l, sectoral, 0.0))
+            by_degree[pl.ds(pl.multiple_of(l * ROWS16, ROWS16), ROWS16), :] = current
+            before, earlier = current, before
+        return before, earlier
+
+    zeros = jnp.zeros(shape, F32)
+    lax.fori_loop(0, LL // 8, block, (zeros, zeros))
+    for i in range(NLAT):
+        by_order[pl.ds(i, LL, stride=ROWS16), :] = by_degree[pl.ds(i, LL, stride=ROWS16), :].T
+
+
+def pair_weights(by_order, first, arrange):
+    second = jnp.where(first == 0, LL // 2, LL - first)
+    at = lambda m: arrange(by_order[pl.ds(pl.multiple_of(m * ROWS16, ROWS16), ROWS16), :])
+    va, vb = at(first), at(second)
+    na, nb = LL - first, LL - second
+    lane = lax.broadcasted_iota(jnp.int32, va.shape, 1)
+    wrap = lambda s: lax.bitwise_and(s, LL - 1)
+    sines = pltpu.roll(va, wrap(2 * na), 1)
+    real = first > 0
+    begin = wrap(2 * na)
+    return (
+        (pltpu.roll(va, wrap(na), 1), None),
+        (
+            jnp.where((lane >= na) & real, sines, 0.0),
+            jnp.where((lane < na) & real, sines, 0.0),
+        ),
+        (None, pltpu.roll(vb, wrap(nb + begin), 1)),
+        (None, pltpu.roll(vb, wrap(2 * nb + begin), 1)),
+    )
+
+
+def order_sums_kernel(
+    row_pairs, col_pairs, steps, orders, cov, *refs
+):
+    outs = refs[: CHUNKS * CHIPS]
+    held, by_degree, by_order, row_w, row_wb, col_w, col_hi, col_lo, sems = refs[CHUNKS * CHIPS :]
+    row_place, col_place = lax.axis_index("row"), lax.axis_index("col")
+    chip = row_place // 2
+    copy = lambda s: pltpu.make_async_copy(
+        cov.at[:, pl.ds(pl.multiple_of(s * STEP, STEP), STEP)], held.at[s], sems.at[s]
+    )
+    for s in range(steps):
+        copy(s).start()
+    legendre_table(by_degree, by_order)
+    row_w[...] = jnp.zeros_like(row_w)
+    col_w[...] = jnp.zeros_like(col_w)
+
+    def own_first(v):
+        place = lax.broadcasted_iota(jnp.int32, v.shape, 0)
+        for bit in (1, 2):
+            up = pltpu.roll(v, ROWS16 - bit, 0)
+            down = pltpu.roll(v, bit, 0)
+            swapped = jnp.where(lax.bitwise_and(place, bit) == 0, up, down)
+            v = jnp.where(lax.bitwise_and(chip, bit) == 0, v, swapped)
+        return v
+
+    for p in range(row_pairs):
+        first = orders[row_place * row_pairs + p]
+        for k, halves in enumerate(pair_weights(by_order, first, own_first)):
+            for h, v in enumerate(halves):
+                if v is not None:
+                    row_w[2 * p + h, pl.ds(p * KEYS + k, NLAT, stride=row_pairs * KEYS), :] = v[
+                        :NLAT
+                    ]
+    for h in range(2 * row_pairs):
+        row_wb[:, h * LL : (h + 1) * LL] = row_w[h].astype(BF16)
+    for p in range(col_pairs):
+        first = orders[col_place * col_pairs + p]
+        s, e = p // 2, p % 2
+        for k, halves in enumerate(pair_weights(by_order, first, lambda v: v)):
+            for h, v in enumerate(halves):
+                if v is not None:
+                    col_w[
+                        2 * e + h,
+                        pl.ds(s * NLAT * 2 * KEYS + e * KEYS + k, NLAT, stride=2 * KEYS),
+                        :,
+                    ] = v[:NLAT]
+    for h in range(4):
+        high, low = split(col_w[h])
+        col_hi[:, h * LL : (h + 1) * LL] = high
+        col_lo[:, h * LL : (h + 1) * LL] = low
+
+    rows = NLAT * 2 * KEYS
+
+    def step(s, carry):
+        copy(s).wait()
+        first = jnp.dot(row_wb[...], held[s], preferred_element_type=F32)
+        own = pl.ds(pl.multiple_of(s * rows, rows), rows)
+        second = dot3((col_hi[own, :], col_lo[own, :]), split(first), ((1,), (1,)))
+        for t in range(CHUNKS):
+            for g in range(NLAT // 4):
+                parts = [
+                    second[8 * (4 * g + u) : 8 * (4 * g + u + 1), LL * t : LL * (t + 1)]
+                    for u in range(4)
+                ]
+                for d, part in enumerate(turn4(parts)):
+                    outs[t * CHIPS + d][
+                        pl.ds(pl.multiple_of(s * 8, 8), 8), pl.ds(g * LL, LL)
+                    ] = part
+        return carry
+
+    lax.fori_loop(0, steps, step, 0)
+
+
+def order_sums(covariance, orders):
+    rows_dev, cols_dev = covariance.shape
+    row_pairs, col_pairs, steps = rows_dev // PAIR, cols_dev // PAIR, cols_dev // STEP
+    lanes = NLAT * row_pairs * KEYS
+    out = jax.ShapeDtypeStruct((col_pairs * KEYS, lanes), F32)
+    return pl.pallas_call(
+        functools.partial(order_sums_kernel, row_pairs, col_pairs, steps),
+        out_shape=[out] * (CHUNKS * CHIPS),
+        in_specs=[pl.BlockSpec(memory_space=pltpu.SMEM), pl.BlockSpec(memory_space=pl.ANY)],
+        out_specs=[pl.BlockSpec(memory_space=pltpu.VMEM)] * (CHUNKS * CHIPS),
+        scratch_shapes=[
+            pltpu.VMEM((steps, rows_dev, STEP), BF16),
+            pltpu.VMEM((LL * ROWS16, LL), F32),
+            pltpu.VMEM((LL * ROWS16, LL), F32),
+            pltpu.VMEM((rows_dev // LL, lanes, LL), F32),
+            pltpu.VMEM((lanes, rows_dev), BF16),
+            pltpu.VMEM((STEP // LL, steps * NLAT * 2 * KEYS, LL), F32),
+            pltpu.VMEM((steps * NLAT * 2 * KEYS, STEP), BF16),
+            pltpu.VMEM((steps * NLAT * 2 * KEYS, STEP), BF16),
+            pltpu.SemaphoreType.DMA((steps,)),
+        ],
+        compiler_params=pltpu.CompilerParams(vmem_limit_bytes=56 * 1024 * 1024),
+        cost_estimate=pl.CostEstimate(
+            flops=2 * lanes * rows_dev * cols_dev,
+            bytes_accessed=2 * rows_dev * cols_dev,
+            transcendentals=0,
+        ),
+        name="order_sums",
+    )(orders, covariance)
+
+
+def columns_kernel(own, near, outer, far, table, result, partial, rhs):
+    for s, ref in enumerate((own, near, outer, far)):
+        n = ref.shape[0]
+        rhs[s * n : (s + 1) * n, :] = ref[...]
+    both = dot3(split(table[...]), split(rhs[...]), ((1,), (0,)))
+    n = result.shape[0]
+    result[...] = both[:n]
+    partial[...] = both[n:]
+
+
+def columns(own, near, outer, far, table):
+    n, lanes = table.shape[0] // 2, own.shape[1]
+    out = jax.ShapeDtypeStruct((n, lanes), F32)
+    return pl.pallas_call(
+        columns_kernel,
+        out_shape=[out, out],
+        in_specs=[pl.BlockSpec(memory_space=pltpu.VMEM)] * 5,
+        out_specs=[pl.BlockSpec(memory_space=pltpu.VMEM)] * 2,
+        scratch_shapes=[pltpu.VMEM((4 * own.shape[0], lanes), F32)],
+        compiler_params=pltpu.CompilerParams(vmem_limit_bytes=32 * 1024 * 1024),
+        cost_estimate=pl.CostEstimate(
+            flops=6 * table.size * lanes, bytes_accessed=16 * own.size, transcendentals=0
+        ),
+        name="columns",
+    )(own, near, outer, far, table)
+
+
+def rows_kernel(mine, other, table, *refs):
+    outs, turned = refs[:CHIPS], refs[CHIPS]
+    n, lanes = mine.shape
+    part = lanes // CHIPS
+    for c, ref in enumerate((mine, other)):
+        for g in range(NLAT // 4):
+            xs = [ref[:, d * part + g * LL : d * part + (g + 1) * LL] for d in range(CHIPS)]
+            for u, y in enumerate(turn4(xs)):
+                turned[c, pl.ds(4 * g + u, n, stride=NLAT), :] = y
+    values = jnp.concatenate([turned[0], turned[1]], axis=1)
+    grid = dot3(split(table[...]), split(values), ((1,), (1,)))
+    m = table.shape[0] // CHIPS
+    for d in range(CHIPS):
+        outs[d][...] = grid[d * m : (d + 1) * m]
+
+
+def rows(mine, other, table):
+    n, lanes = mine.shape
+    m = table.shape[0] // CHIPS
+    out = jax.ShapeDtypeStruct((m, n * NLAT), F32)
+    return pl.pallas_call(
+        rows_kernel,
+        out_shape=[out] * CHIPS,
+        in_specs=[pl.BlockSpec(memory_space=pltpu.VMEM)] * 3,
+        out_specs=[pl.BlockSpec(memory_space=pltpu.VMEM)] * CHIPS,
+        scratch_shapes=[pltpu.VMEM((2, n * NLAT, LL), F32)],
+        compiler_params=pltpu.CompilerParams(vmem_limit_bytes=32 * 1024 * 1024),
+        cost_estimate=pl.CostEstimate(
+            flops=6 * table.size * n * NLAT, bytes_accessed=16 * mine.size, transcendentals=0
+        ),
+        name="rows",
+    )(mine, other, table)
+
+
+def place_kernel(*refs):
+    parts, out, held = refs[:-2], refs[-2], refs[-1]
+    tiles = held.shape[0]
+    chip = lax.axis_index("row") // 2
+    for t in range(CHUNKS):
+        for d in range(CHIPS):
+            ref = parts[t * CHIPS + d]
+            row = 4 * t + lax.bitwise_xor(chip, d)
+            for h in range(tiles):
+                held[h, pl.ds(row, ref.shape[0], stride=NLAT), :] = ref[:, h * LL : (h + 1) * LL]
+    for h in range(tiles):
+        out[:, h * LL : (h + 1) * LL] = held[h]
+
+
+def place(parts):
+    m, lanes = parts[0].shape
+    return pl.pallas_call(
+        place_kernel,
+        out_shape=jax.ShapeDtypeStruct((m * NLAT, lanes), F32),
+        in_specs=[pl.BlockSpec(memory_space=pltpu.VMEM)] * len(parts),
+        out_specs=pl.BlockSpec(memory_space=pltpu.VMEM),
+        scratch_shapes=[pltpu.VMEM((lanes // LL, m * NLAT, LL), F32)],
+        compiler_params=pltpu.CompilerParams(vmem_limit_bytes=32 * 1024 * 1024),
+        name="place",
+    )(*parts)
+
+
+def wave(lons, keys):
+    turns = (lons[:, None] * (keys // 2)[None, :] + (NLON // 4) * (1 - keys % 2)[None, :]) % NLON
+    return jnp.sin(turns.astype(F32) * (2.0 * math.pi / NLON))
+
+
+def tables(orders):
+    row_place, col_place = lax.axis_index("row"), lax.axis_index("col")
+    row_count, col_count = lax.axis_size("row"), lax.axis_size("col")
+    second = jnp.where(orders == 0, LL // 2, LL - orders)
+    keys = jnp.stack([2 * orders, 2 * orders + 1, 2 * second, 2 * second + 1], 1).reshape(-1)
+    by_col = keys.reshape(col_count, -1)
+    pick = lambda table, index: lax.dynamic_index_in_dim(table, index, 0, keepdims=False)
+    col_keys = jnp.concatenate([pick(by_col, col_place ^ s) for s in (0, 3, 1, 2)])
+    lons = jnp.arange(NLON // col_count, dtype=jnp.int32)
+    col_lons = jnp.concatenate([lons + (col_place ^ s) * lons.size for s in (0, 1)])
+    col_table = wave(col_lons, col_keys)
+    n = by_col.shape[1]
+    hidden = (jnp.arange(2 * lons.size) >= lons.size)[:, None] & (
+        (jnp.arange(4 * n) // n) == 2
+    )[None, :]
+    col_table = jnp.where(hidden, 0.0, col_table)
+    by_row = keys.reshape(row_count, -1)
+    row_keys = jnp.concatenate(
+        [pick(by_row, row_place ^ (2 * d + c)) for c in range(2) for d in range(CHIPS)]
+    )
+    lons = jnp.arange(NLON // row_count, dtype=jnp.int32)
+    row_lons = jnp.concatenate(
+        [lons + (row_place ^ (2 * d)) * lons.size for d in range(CHIPS)]
+    )
+    return col_table, wave(row_lons, row_keys)
+
+
+def chunked(covariance, coef_index):
+    orders = coef_index[1].reshape(-1, PAIR)[:, 0]
+    sums = order_sums(covariance, orders)
+    orders, *sums = lax.optimization_barrier((orders, *sums))
+    col_table, row_table = tables(orders)
+    flip = lambda x, bits: lax.ppermute(
+        x, "row", [(r, r ^ bits) for r in range(lax.axis_size("row"))]
+    )
+    along = lambda x, *pairs: lax.ppermute(x, "col", pairs)
+    parts = []
+    for t in range(CHUNKS):
+        mine = sums[t * CHIPS : (t + 1) * CHIPS]
+        own = jnp.concatenate(
+            [mine[0]] + [flip(mine[d], 2 * d) for d in range(1, CHIPS)], axis=1
+        )
+        near = along(own, (1, 2), (2, 1))
+        outer = along(own, (0, 1), (3, 2))
+        far = along(outer, (1, 2), (2, 1))
+        result, partial = columns(own, near, outer, far, col_table)
+        result = result + along(partial, (1, 0), (2, 3))
+        grid = rows(result, flip(result, 1), row_table)
+        parts += [grid[0]] + [flip(grid[d], 2 * d) for d in range(1, CHIPS)]
+    return place(parts)
 
 
 def legendre_rows(lat_count, lon_count, degree_count):
@@ -136,6 +492,7 @@
 def solution(mesh):
     in_specs = (P("row", "col"), P())
     out_specs = P("row", "col")
+    fits = mesh.shape["row"] == 2 * CHIPS and mesh.shape["col"] == 4
     return jax.shard_map(
-        on_device, mesh=mesh, in_specs=in_specs, out_specs=out_specs, check_vma=False
-    )
+        chunked if fits else on_device, mesh=mesh, in_specs=in_specs, out_specs=out_specs, check_vma=False
+    )

time: 708 us -> 144 us (0.20); the launches traced: 697 us -> 143 us
  other arithmetic: 192 us -> 4.31 us
  waiting for transfers between devices: 251 us -> 64.9 us
  local copies, waits for them, and re-layouts: 99.1 us -> 4.92 us
  loops' own time: 83 us -> 0 us
  matrix products: 48.9 us -> 0 us
  starting transfers between devices: 9.12 us -> 43.1 us
  Pallas kernels: 0 us -> 25.5 us
  between operations: 14.1 us -> 0.45 us
    reduce_scatter x1 -> x0, waiting for transfers between devices: 199 us -> none  [on_device(): lax.psum_scatter(grid_vals.reshape(pts_col * lax.axis_size('col'), pts_ro...]
    sqrt x128 -> x0, other arithmetic: 83.6 us -> none  [advance(): jnp.sqrt(jnp.maximum((2.0 * degree + 1.0) * (deg_sum - 1.0) * (deg_diff -...]
    another operation x1 -> x0, loops' own time: 83 us -> none  [legendre_rows(): lax.scan(advance, start_pair, jnp.arange(degree_count, dtype=jnp.float32)...]
    lt x128 -> x0, other arithmetic: 82 us -> none  [advance(): orders < degree]
    ppermute x0 -> x33, waiting for transfers between devices: none -> 64.9 us  [the longest x12 47.4 us: chunked(): along = lambda x, *pairs: lax.ppermute(x, 'col', pairs)]
    all_to_all x2 -> x0, waiting for transfers between devices: 52.7 us -> none  [the longest x1 36.6 us: on_device(): lax.all_to_all(grid_vals, 'row', split_axis=0, concat_axis=2, tiled=True)]
    dot_general x3 -> x0, matrix products: 45.2 us -> none  [the longest x1 20.4 us: on_device(): jnp.einsum('ak,jbk->ajb', first_pass, col_weights, precision=lax.Precisio...]
    ppermute x0 -> x33, starting transfers between devices: none -> 43.1 us  [the longest x21 24.6 us: chunked(): lax.ppermute(x, 'row', [(r, r ^ bits) for r in range(lax.axis_size('row'))])]
  transfers between devices with their start and end apart: 3 -> 33, of which waited for: 3 -> 12; matrix products, arithmetic and copies ran while one was open for 0% -> 5% of each run, Pallas kernels for 0% -> 4%
where the time goes in v1:
time: 144 us; the launch traced here: 143 us
  waiting for transfers between devices  64.9 us (45%)
  starting transfers between devices  43.1 us (30%)
  Pallas kernels  25.5 us (18%)
  local copies, waits for them, and re-layouts  4.92 us (3%)
  other arithmetic  4.31 us (3%)
    ppermute x12, waiting for transfers between devices, chunked(): along = lambda x, *pairs: lax.ppermute(x, 'col', pairs)  47.4 us
    ppermute x21, starting transfers between devices, chunked(): lax.ppermute(x, 'row', [(r, r ^ bits) for r in range(lax.axis_size('row'))])  24.6 us
    ppermute x12, starting transfers between devices, chunked(): along = lambda x, *pairs: lax.ppermute(x, 'col', pairs)  18.4 us
    pallas_call x1, Pallas kernels, order_sums(): pl.pallas_call(functools.partial(order_sums_kernel, row_pairs, col_pairs,...  17.7 us
    ppermute x21, waiting for transfers between devices, chunked(): lax.ppermute(x, 'row', [(r, r ^ bits) for r in range(lax.axis_size('row'))])  17.6 us
    pallas_call x3, Pallas kernels, rows(): pl.pallas_call(rows_kernel, out_shape=[out] * CHIPS, in_specs=[pl.BlockSp...  3.91 us
    unnamed x12, local copies, waits for them, and re-layouts  3.35 us
  transfers between devices with their start and end apart: 33, of which 12 were waited for; matrix products, arithmetic and copies ran while one was open for 5% of the time, Pallas kernels for 4%

profile of v1, /device:TPU:0, one launch (start us, length us, event | category | flops | bytes accessed | tf_op | source)
XLA Modules:
  0.0 143.2 jit_solution(18046360604210860629)
XLA Ops:
  1.8 17.7 %order_sums.1 = (f32[64,384]{1,0:T(8,128)}, f32[64,384]{1,0:T(8,128)}, f32[64,384]{1,0:T(8,128)}, f32[64,384]{1,0:T(8,128)}, f32[64,384]{1,0:T(8,128)}, /*index=...) custom-call(s32[64]{0:T(128)} %bitcast.33, ...), custom_call_target="tpu_custom_call" | custom-call | flops 6442450944 | bytes 16777216 | tf_op jit(solution)/shard_map/order_sums/pallas_call | solution.py:198
  19.5 3.0 %collective-permute-start.22 = (f32[64,384]{1,0:T(8,128)}, f32[64,384]{1,0:T(8,128)S(1)}, u32[]{:S(2)}, u32[]{:S(2)}) collective-permute-start(f32[64,384]{1,0:T(8,128)} %get-tuple-element.82), channel_id=1, source_target_pairs={{0,8},{4,12},{8,0},{12,4},{16,24},{20,28},{24,16},{28,20},{1,9},{5... | collective-permute-start | bytes 294920 | tf_op jit(solution)/shard_map/ppermute | solution.py:349
  22.5 1.5 %collective-permute-start.23 = (f32[64,384]{1,0:T(8,128)}, f32[64,384]{1,0:T(8,128)S(1)}, u32[]{:S(2)}, u32[]{:S(2)}) collective-permute-start(f32[64,384]{1,0:T(8,128)} %get-tuple-element.83), channel_id=1, source_target_pairs={{0,16},{4,20},{8,24},{12,28},{16,0},{20,4},{24,8},{28,12},{1,17},{... | collective-permute-start | bytes 294920 | tf_op jit(solution)/shard_map/ppermute | solution.py:349
  24.0 1.9 %collective-permute-start.11 = (f32[64,384]{1,0:T(8,128)}, f32[64,384]{1,0:T(8,128)S(1)}, u32[]{:S(2)}, u32[]{:S(2)}) collective-permute-start(f32[64,384]{1,0:T(8,128)} %get-tuple-element.72), channel_id=1, source_target_pairs={{0,8},{4,12},{8,0},{12,4},{16,24},{20,28},{24,16},{28,20},{1,9},{5... | collective-permute-start | bytes 294920 | tf_op jit(solution)/shard_map/ppermute | solution.py:349
  25.9 1.5 %collective-permute-start.12 = (f32[64,384]{1,0:T(8,128)}, f32[64,384]{1,0:T(8,128)S(1)}, u32[]{:S(2)}, u32[]{:S(2)}) collective-permute-start(f32[64,384]{1,0:T(8,128)} %get-tuple-element.73), channel_id=1, source_target_pairs={{0,16},{4,20},{8,24},{12,28},{16,0},{20,4},{24,8},{28,12},{1,17},{... | collective-permute-start | bytes 294920 | tf_op jit(solution)/shard_map/ppermute | solution.py:349
  30.8 2.0 %collective-permute-start = (f32[64,384]{1,0:T(8,128)}, f32[64,384]{1,0:T(8,128)S(1)}, u32[]{:S(2)}, u32[]{:S(2)}) collective-permute-start(f32[64,384]{1,0:T(8,128)} %get-tuple-element.61), channel_id=1, source_target_pairs={{0,8},{4,12},{8,0},{12,4},{16,24},{20,28},{24,16},{28,20},{1,9},{5... | collective-permute-start | bytes 294920 | tf_op jit(solution)/shard_map/ppermute | solution.py:349
  32.8 1.6 %collective-permute-start.1 = (f32[64,384]{1,0:T(8,128)}, f32[64,384]{1,0:T(8,128)S(1)}, u32[]{:S(2)}, u32[]{:S(2)}) collective-permute-start(f32[64,384]{1,0:T(8,128)} %get-tuple-element.62), channel_id=1, source_target_pairs={{0,16},{4,20},{8,24},{12,28},{16,0},{20,4},{24,8},{28,12},{1,17},{... | collective-permute-start | bytes 294920 | tf_op jit(solution)/shard_map/ppermute | solution.py:349
  34.6 4.0 %collective-permute-start.26 = (f32[64,1536]{1,0:T(8,128)S(1)}, f32[64,1536]{1,0:T(8,128)S(1)}, u32[]{:S(2)}, u32[]{:S(2)}) collective-permute-start(f32[64,1536]{1,0:T(8,128)S(1)} %constant_dynamic-update-slice_fusion.8.own), channel_id=1, source_target_pairs={{0,1},{3,2},{4,5},{7,6},{8,9},{11,10},{12,13},{15,14},{16,17},{19,... | collective-permute-start | bytes 1179656 | tf_op jit(solution)/shard_map/ppermute | solution.py:352
  39.3 5.0 %collective-permute-start.15 = (f32[64,1536]{1,0:T(8,128)S(1)}, f32[64,1536]{1,0:T(8,128)S(1)}, u32[]{:S(2)}, u32[]{:S(2)}) collective-permute-start(f32[64,1536]{1,0:T(8,128)S(1)} %constant_dynamic-update-slice_fusion.4.own), channel_id=1, source_target_pairs={{0,1},{3,2},{4,5},{7,6},{8,9},{11,10},{12,13},{15,14},{16,17},{19,... | collective-permute-start | bytes 1179656 | tf_op jit(solution)/shard_map/ppermute | solution.py:352
  46.4 1.6 %collective-permute-done.26.outer = f32[64,1536]{1,0:T(8,128)S(1)} collective-permute-done((f32[64,1536]{1,0:T(8,128)S(1)}, f32[64,1536]{1,0:T(8,128)S(1)}, u32[]{:S(2)}, u32[]{:S(2)}) %collective-permute-start.26) | collective-permute-done | bytes 393248 | tf_op jit(solution)/shard_map/ppermute | solution.py:352
  48.7 7.7 %collective-permute-done.15.outer = f32[64,1536]{1,0:T(8,128)S(1)} collective-permute-done((f32[64,1536]{1,0:T(8,128)S(1)}, f32[64,1536]{1,0:T(8,128)S(1)}, u32[]{:S(2)}, u32[]{:S(2)}) %collective-permute-start.15) | collective-permute-done | bytes 393248 | tf_op jit(solution)/shard_map/ppermute | solution.py:352
  57.9 3.3 %collective-permute-done.4.outer = f32[64,1536]{1,0:T(8,128)S(1)} collective-permute-done((f32[64,1536]{1,0:T(8,128)S(1)}, f32[64,1536]{1,0:T(8,128)S(1)}, u32[]{:S(2)}, u32[]{:S(2)}) %collective-permute-start.4) | collective-permute-done | bytes 393248 | tf_op jit(solution)/shard_map/ppermute | solution.py:352
  68.8 16.2 %collective-permute-done.28 = f32[96,1536]{1,0:T(8,128)S(1)} collective-permute-done((f32[96,1536]{1,0:T(8,128)S(1)}, f32[96,1536]{1,0:T(8,128)S(1)}, u32[]{:S(2)}, u32[]{:S(2)}) %collective-permute-start.28) | collective-permute-done | bytes 589856 | tf_op jit(solution)/shard_map/ppermute | solution.py:352
  85.2 8.3 %collective-permute-done.17 = f32[96,1536]{1,0:T(8,128)} collective-permute-done((f32[96,1536]{1,0:T(8,128)S(1)}, f32[96,1536]{1,0:T(8,128)}, u32[]{:S(2)}, u32[]{:S(2)}) %collective-permute-start.17) | collective-permute-done | bytes 589856 | tf_op jit(solution)/shard_map/ppermute | solution.py:352
  94.8 10.2 %collective-permute-done.6 = f32[96,1536]{1,0:T(8,128)} collective-permute-done((f32[96,1536]{1,0:T(8,128)S(1)}, f32[96,1536]{1,0:T(8,128)}, u32[]{:S(2)}, u32[]{:S(2)}) %collective-permute-start.6) | collective-permute-done | bytes 589856 | tf_op jit(solution)/shard_map/ppermute | solution.py:352
  108.4 1.6 %collective-permute-start.30 = (f32[48,1152]{1,0:T(8,128)S(1)}, f32[48,1152]{1,0:T(8,128)S(1)}, u32[]{:S(2)}, u32[]{:S(2)}) collective-permute-start(f32[48,1152]{1,0:T(8,128)S(1)} %get-tuple-element.88), channel_id=1, source_target_pairs={{0,8},{4,12},{8,0},{12,4},{16,24},{20,28},{24,16},{28,20},{1,9},{5... | collective-permute-start | bytes 663560 | tf_op jit(solution)/shard_map/ppermute | solution.py:349
  109.9 1.5 %collective-permute-start.31 = (f32[48,1152]{1,0:T(8,128)S(1)}, f32[48,1152]{1,0:T(8,128)S(1)}, u32[]{:S(2)}, u32[]{:S(2)}) collective-permute-start(f32[48,1152]{1,0:T(8,128)S(1)} %get-tuple-element.89), channel_id=1, source_target_pairs={{0,16},{4,20},{8,24},{12,28},{16,0},{20,4},{24,8},{28,12},{1,17},{... | collective-permute-start | bytes 663560 | tf_op jit(solution)/shard_map/ppermute | solution.py:349
  113.3 1.6 %collective-permute-start.19 = (f32[48,1152]{1,0:T(8,128)S(1)}, f32[48,1152]{1,0:T(8,128)S(1)}, u32[]{:S(2)}, u32[]{:S(2)}) collective-permute-start(f32[48,1152]{1,0:T(8,128)S(1)} %get-tuple-element.78), channel_id=1, source_target_pairs={{0,8},{4,12},{8,0},{12,4},{16,24},{20,28},{24,16},{28,20},{1,9},{5... | collective-permute-start | bytes 663560 | tf_op jit(solution)/shard_map/ppermute | solution.py:349
  119.1 3.8 %collective-permute-done.31.refs_10_ = f32[48,1152]{1,0:T(8,128)S(1)} collective-permute-done((f32[48,1152]{1,0:T(8,128)S(1)}, f32[48,1152]{1,0:T(8,128)S(1)}, u32[]{:S(2)}, u32[]{:S(2)}) %collective-permute-start.31) | collective-permute-done | bytes 221216 | tf_op jit(solution)/shard_map/ppermute | solution.py:349
  124.4 1.6 %collective-permute-start.8 = (f32[48,1152]{1,0:T(8,128)S(1)}, f32[48,1152]{1,0:T(8,128)S(1)}, u32[]{:S(2)}, u32[]{:S(2)}) collective-permute-start(f32[48,1152]{1,0:T(8,128)S(1)} %get-tuple-element.68), channel_id=1, source_target_pairs={{0,8},{4,12},{8,0},{12,4},{16,24},{20,28},{24,16},{28,20},{1,9},{5... | collective-permute-start | bytes 663560 | tf_op jit(solution)/shard_map/ppermute | solution.py:349
  126.2 1.5 %collective-permute-start.9 = (f32[48,1152]{1,0:T(8,128)S(1)}, f32[48,1152]{1,0:T(8,128)S(1)}, u32[]{:S(2)}, u32[]{:S(2)}) collective-permute-start(f32[48,1152]{1,0:T(8,128)S(1)} %get-tuple-element.69), channel_id=1, source_target_pairs={{0,16},{4,20},{8,24},{12,28},{16,0},{20,4},{24,8},{28,12},{1,17},{... | collective-permute-start | bytes 663560 | tf_op jit(solution)/shard_map/ppermute | solution.py:349
  127.7 8.6 %collective-permute-done.20.refs_6_ = f32[48,1152]{1,0:T(8,128)S(1)} collective-permute-done((f32[48,1152]{1,0:T(8,128)S(1)}, f32[48,1152]{1,0:T(8,128)S(1)}, u32[]{:S(2)}, u32[]{:S(2)}) %collective-permute-start.20) | collective-permute-done | bytes 221216 | tf_op jit(solution)/shard_map/ppermute | solution.py:349
  136.7 3.4 %collective-permute-done.8.refs_1_ = f32[48,1152]{1,0:T(8,128)S(1)} collective-permute-done((f32[48,1152]{1,0:T(8,128)S(1)}, f32[48,1152]{1,0:T(8,128)S(1)}, u32[]{:S(2)}, u32[]{:S(2)}) %collective-permute-start.8) | collective-permute-done | bytes 221216 | tf_op jit(solution)/shard_map/ppermute | solution.py:349
  141.2 2.1 %place.1 = f32[576,1152]{1,0:T(8,128)} custom-call(f32[48,1152]{1,0:T(8,128)S(1)} %get-tuple-element.67.refs_0_, f32[48,1152]{1,0:T(8,128)S(1)} %collective-permute-done.8.refs_1_, f32[48,1152]{1,0:T(8,128)S(1)} %collective-permute-done.9.refs_2_, f32[48,1152]{1,0:T(8,128)S(1)} %collective-permute-done.10.refs_3_, f32[48,1152]{1,0:T(8,128)S(1)} %get-tuple-element.77.refs_4_, ...), custom_call_target="tpu_custom_call" | custom-call | tf_op jit(solution)/shard_map/place/pallas_call | solution.py:301
  (90 shorter events, 31.6 us)
Async XLA Ops:
  19.5 11.2 %collective-permute-start.22 = (f32[64,384]{1,0:T(8,128)}, f32[64,384]{1,0:T(8,128)S(1)}, u32[]{:S(2)}, u32[]{:S(2)}) collective-permute-start(f32[64,384]{1,0:T(8,128)} %get-tuple-element.82), channel_id=1, source_target_pairs={{0,8},{4,12},{8,0},{12,4},{16,24},{20,28},{24,16},{28,20},{1,9},{5... | collective-permute-start | bytes 294920 | tf_op jit(solution)/shard_map/ppermute | solution.py:349
  24.0 10.5 %collective-permute-start.11 = (f32[64,384]{1,0:T(8,128)}, f32[64,384]{1,0:T(8,128)S(1)}, u32[]{:S(2)}, u32[]{:S(2)}) collective-permute-start(f32[64,384]{1,0:T(8,128)} %get-tuple-element.72), channel_id=1, source_target_pairs={{0,8},{4,12},{8,0},{12,4},{16,24},{20,28},{24,16},{28,20},{1,9},{5... | collective-permute-start | bytes 294920 | tf_op jit(solution)/shard_map/ppermute | solution.py:349
  32.8 11.5 %collective-permute-start.1 = (f32[64,384]{1,0:T(8,128)}, f32[64,384]{1,0:T(8,128)S(1)}, u32[]{:S(2)}, u32[]{:S(2)}) collective-permute-start(f32[64,384]{1,0:T(8,128)} %get-tuple-element.62), channel_id=1, source_target_pairs={{0,16},{4,20},{8,24},{12,28},{16,0},{20,4},{24,8},{28,12},{1,17},{... | collective-permute-start | bytes 294920 | tf_op jit(solution)/shard_map/ppermute | solution.py:349
  34.5 9.9 %collective-permute-start.2 = (f32[64,384]{1,0:T(8,128)}, f32[64,384]{1,0:T(8,128)S(1)}, u32[]{:S(2)}, u32[]{:S(2)}) collective-permute-start(f32[64,384]{1,0:T(8,128)} %get-tuple-element.63), channel_id=1, source_target_pairs={{0,24},{4,28},{8,16},{12,20},{16,8},{20,12},{24,0},{28,4},{1,25},{... | collective-permute-start | bytes 294920 | tf_op jit(solution)/shard_map/ppermute | solution.py:349
  34.6 13.5 %collective-permute-start.26 = (f32[64,1536]{1,0:T(8,128)S(1)}, f32[64,1536]{1,0:T(8,128)S(1)}, u32[]{:S(2)}, u32[]{:S(2)}) collective-permute-start(f32[64,1536]{1,0:T(8,128)S(1)} %constant_dynamic-update-slice_fusion.8.own), channel_id=1, source_target_pairs={{0,1},{3,2},{4,5},{7,6},{8,9},{11,10},{12,13},{15,14},{16,17},{19,... | collective-permute-start | bytes 1179656 | tf_op jit(solution)/shard_map/ppermute | solution.py:352
  38.6 18.7 %collective-permute-start.25 = (f32[64,1536]{1,0:T(8,128)S(1)}, f32[64,1536]{1,0:T(8,128)S(1)}, u32[]{:S(2)}, u32[]{:S(2)}) collective-permute-start(f32[64,1536]{1,0:T(8,128)S(1)} %constant_dynamic-update-slice_fusion.8.own), channel_id=1, source_target_pairs={{1,2},{2,1},{5,6},{6,5},{9,10},{10,9},{13,14},{14,13},{17,18},{18,... | collective-permute-start | bytes 1179656 | tf_op jit(solution)/shard_map/ppermute | solution.py:352
  39.3 17.2 %collective-permute-start.15 = (f32[64,1536]{1,0:T(8,128)S(1)}, f32[64,1536]{1,0:T(8,128)S(1)}, u32[]{:S(2)}, u32[]{:S(2)}) collective-permute-start(f32[64,1536]{1,0:T(8,128)S(1)} %constant_dynamic-update-slice_fusion.4.own), channel_id=1, source_target_pairs={{0,1},{3,2},{4,5},{7,6},{8,9},{11,10},{12,13},{15,14},{16,17},{19,... | collective-permute-start | bytes 1179656 | tf_op jit(solution)/shard_map/ppermute | solution.py:352
  44.4 16.8 %collective-permute-start.4 = (f32[64,1536]{1,0:T(8,128)S(1)}, f32[64,1536]{1,0:T(8,128)S(1)}, u32[]{:S(2)}, u32[]{:S(2)}) collective-permute-start(f32[64,1536]{1,0:T(8,128)S(1)} %constant_dynamic-update-slice_fusion.own), channel_id=1, source_target_pairs={{0,1},{3,2},{4,5},{7,6},{8,9},{11,10},{12,13},{15,14},{16,17},{19,... | collective-permute-start | bytes 1179656 | tf_op jit(solution)/shard_map/ppermute | solution.py:352
  45.8 18.9 %collective-permute-start.14 = (f32[64,1536]{1,0:T(8,128)S(1)}, f32[64,1536]{1,0:T(8,128)S(1)}, u32[]{:S(2)}, u32[]{:S(2)}) collective-permute-start(f32[64,1536]{1,0:T(8,128)S(1)} %constant_dynamic-update-slice_fusion.4.own), channel_id=1, source_target_pairs={{1,2},{2,1},{5,6},{6,5},{9,10},{10,9},{13,14},{14,13},{17,18},{18,... | collective-permute-start | bytes 1179656 | tf_op jit(solution)/shard_map/ppermute | solution.py:352
  48.1 14.7 %collective-permute-start.27 = (f32[64,1536]{1,0:T(8,128)S(1)}, f32[64,1536]{1,0:T(8,128)S(1)}, u32[]{:S(2)}, u32[]{:S(2)}) collective-permute-start(f32[64,1536]{1,0:T(8,128)S(1)} %collective-permute-done.26.outer), channel_id=1, source_target_pairs={{1,2},{2,1},{5,6},{6,5},{9,10},{10,9},{13,14},{14,13},{17,18},{18,... | collective-permute-start | bytes 1179656 | tf_op jit(solution)/shard_map/ppermute | solution.py:352
  57.3 9.4 %collective-permute-start.3 = (f32[64,1536]{1,0:T(8,128)S(1)}, f32[64,1536]{1,0:T(8,128)S(1)}, u32[]{:S(2)}, u32[]{:S(2)}) collective-permute-start(f32[64,1536]{1,0:T(8,128)S(1)} %constant_dynamic-update-slice_fusion.own), channel_id=1, source_target_pairs={{1,2},{2,1},{5,6},{6,5},{9,10},{10,9},{13,14},{14,13},{17,18},{18,... | collective-permute-start | bytes 1179656 | tf_op jit(solution)/shard_map/ppermute | solution.py:352
  63.4 21.7 %collective-permute-start.28 = (f32[96,1536]{1,0:T(8,128)S(1)}, f32[96,1536]{1,0:T(8,128)S(1)}, u32[]{:S(2)}, u32[]{:S(2)}) collective-permute-start(f32[96,1536]{1,0:T(8,128)S(1)} %get-tuple-element.86), channel_id=1, source_target_pairs={{1,0},{2,3},{5,4},{6,7},{9,8},{10,11},{13,12},{14,15},{17,16},{18,... | collective-permute-start | bytes 1769480 | tf_op jit(solution)/shard_map/ppermute | solution.py:352
  65.4 28.2 %collective-permute-start.17 = (f32[96,1536]{1,0:T(8,128)S(1)}, f32[96,1536]{1,0:T(8,128)}, u32[]{:S(2)}, u32[]{:S(2)}) collective-permute-start(f32[96,1536]{1,0:T(8,128)S(1)} %get-tuple-element.76), channel_id=1, source_target_pairs={{1,0},{2,3},{5,4},{6,7},{9,8},{10,11},{13,12},{14,15},{17,16},{18,... | collective-permute-start | bytes 1769480 | tf_op jit(solution)/shard_map/ppermute | solution.py:352
  67.3 37.6 %collective-permute-start.6 = (f32[96,1536]{1,0:T(8,128)S(1)}, f32[96,1536]{1,0:T(8,128)}, u32[]{:S(2)}, u32[]{:S(2)}) collective-permute-start(f32[96,1536]{1,0:T(8,128)S(1)} %get-tuple-element.66), channel_id=1, source_target_pairs={{1,0},{2,3},{5,4},{6,7},{9,8},{10,11},{13,12},{14,15},{17,16},{18,... | collective-permute-start | bytes 1769480 | tf_op jit(solution)/shard_map/ppermute | solution.py:352
  85.1 22.0 %collective-permute-start.29 = (f32[96,1536]{1,0:T(8,128)S(1)}, f32[96,1536]{1,0:T(8,128)S(1)}, u32[]{:S(2)}, u32[]{:S(2)}) collective-permute-start(f32[96,1536]{1,0:T(8,128)S(1)} %add.184.mine), channel_id=1, source_target_pairs={{0,4},{4,0},{8,12},{12,8},{16,20},{20,16},{24,28},{28,24},{1,5},{5... | collective-permute-start | bytes 1769480 | tf_op jit(solution)/shard_map/ppermute | solution.py:349
  94.7 17.3 %collective-permute-start.18 = (f32[96,1536]{1,0:T(8,128)S(1)}, f32[96,1536]{1,0:T(8,128)S(1)}, u32[]{:S(2)}, u32[]{:S(2)}) collective-permute-start(f32[96,1536]{1,0:T(8,128)S(1)} %add.183.mine), channel_id=1, source_target_pairs={{0,4},{4,0},{8,12},{12,8},{16,20},{20,16},{24,28},{28,24},{1,5},{5... | collective-permute-start | bytes 1769480 | tf_op jit(solution)/shard_map/ppermute | solution.py:349
  109.9 12.9 %collective-permute-start.31 = (f32[48,1152]{1,0:T(8,128)S(1)}, f32[48,1152]{1,0:T(8,128)S(1)}, u32[]{:S(2)}, u32[]{:S(2)}) collective-permute-start(f32[48,1152]{1,0:T(8,128)S(1)} %get-tuple-element.89), channel_id=1, source_target_pairs={{0,16},{4,20},{8,24},{12,28},{16,0},{20,4},{24,8},{28,12},{1,17},{... | collective-permute-start | bytes 663560 | tf_op jit(solution)/shard_map/ppermute | solution.py:349
  111.5 12.9 %collective-permute-start.32 = (f32[48,1152]{1,0:T(8,128)S(1)}, f32[48,1152]{1,0:T(8,128)S(1)}, u32[]{:S(2)}, u32[]{:S(2)}) collective-permute-start(f32[48,1152]{1,0:T(8,128)S(1)} %get-tuple-element.90), channel_id=1, source_target_pairs={{0,24},{4,28},{8,16},{12,20},{16,8},{20,12},{24,0},{28,4},{1,25},{... | collective-permute-start | bytes 663560 | tf_op jit(solution)/shard_map/ppermute | solution.py:349
  113.3 12.9 %collective-permute-start.19 = (f32[48,1152]{1,0:T(8,128)S(1)}, f32[48,1152]{1,0:T(8,128)S(1)}, u32[]{:S(2)}, u32[]{:S(2)}) collective-permute-start(f32[48,1152]{1,0:T(8,128)S(1)} %get-tuple-element.78), channel_id=1, source_target_pairs={{0,8},{4,12},{8,0},{12,4},{16,24},{20,28},{24,16},{28,20},{1,9},{5... | collective-permute-start | bytes 663560 | tf_op jit(solution)/shard_map/ppermute | solution.py:349
  114.8 21.5 %collective-permute-start.20 = (f32[48,1152]{1,0:T(8,128)S(1)}, f32[48,1152]{1,0:T(8,128)S(1)}, u32[]{:S(2)}, u32[]{:S(2)}) collective-permute-start(f32[48,1152]{1,0:T(8,128)S(1)} %get-tuple-element.79), channel_id=1, source_target_pairs={{0,16},{4,20},{8,24},{12,28},{16,0},{20,4},{24,8},{28,12},{1,17},{... | collective-permute-start | bytes 663560 | tf_op jit(solution)/shard_map/ppermute | solution.py:349
  117.6 18.7 %collective-permute-start.21 = (f32[48,1152]{1,0:T(8,128)S(1)}, f32[48,1152]{1,0:T(8,128)S(1)}, u32[]{:S(2)}, u32[]{:S(2)}) collective-permute-start(f32[48,1152]{1,0:T(8,128)S(1)} %get-tuple-element.80), channel_id=1, source_target_pairs={{0,24},{4,28},{8,16},{12,20},{16,8},{20,12},{24,0},{28,4},{1,25},{... | collective-permute-start | bytes 663560 | tf_op jit(solution)/shard_map/ppermute | solution.py:349
  122.9 13.8 %collective-permute-start.10 = (f32[48,1152]{1,0:T(8,128)S(1)}, f32[48,1152]{1,0:T(8,128)S(1)}, u32[]{:S(2)}, u32[]{:S(2)}) collective-permute-start(f32[48,1152]{1,0:T(8,128)S(1)} %get-tuple-element.70), channel_id=1, source_target_pairs={{0,24},{4,28},{8,16},{12,20},{16,8},{20,12},{24,0},{28,4},{1,25},{... | collective-permute-start | bytes 663560 | tf_op jit(solution)/shard_map/ppermute | solution.py:349
  124.4 15.7 %collective-permute-start.8 = (f32[48,1152]{1,0:T(8,128)S(1)}, f32[48,1152]{1,0:T(8,128)S(1)}, u32[]{:S(2)}, u32[]{:S(2)}) collective-permute-start(f32[48,1152]{1,0:T(8,128)S(1)} %get-tuple-element.68), channel_id=1, source_target_pairs={{0,8},{4,12},{8,0},{12,4},{16,24},{20,28},{24,16},{28,20},{1,9},{5... | collective-permute-start | bytes 663560 | tf_op jit(solution)/shard_map/ppermute | solution.py:349
  126.2 15.0 %collective-permute-start.9 = (f32[48,1152]{1,0:T(8,128)S(1)}, f32[48,1152]{1,0:T(8,128)S(1)}, u32[]{:S(2)}, u32[]{:S(2)}) collective-permute-start(f32[48,1152]{1,0:T(8,128)S(1)} %get-tuple-element.69), channel_id=1, source_target_pairs={{0,16},{4,20},{8,24},{12,28},{16,0},{20,4},{24,8},{28,12},{1,17},{... | collective-permute-start | bytes 663560 | tf_op jit(solution)/shard_map/ppermute | solution.py:349
  (10 other events, 99.5 us)

commit v2 on v1

--- a/solution.py
+++ b/solution.py
@@ -20,6 +20,7 @@
 PAIR = 2 * LL
 KEYS = 4
 STEP = 2 * PAIR
+GROUP = 2
 
 
 def split(x):
@@ -117,19 +118,33 @@
     )
 
 
-def order_sums_kernel(
-    row_pairs, col_pairs, steps, orders, cov, *refs
-):
-    outs = refs[: CHUNKS * CHIPS]
-    held, by_degree, by_order, row_w, row_wb, col_w, col_hi, col_lo, sems = refs[CHUNKS * CHIPS :]
+def order_sums_kernel(row_pairs, col_pairs, steps, index, cov, *refs):
+    first_out, later_outs = refs[0], refs[1 : 1 + CHIPS]
+    (
+        held, by_degree, by_order, row_w, row_wb, col_w, col_wb, even, odd, second, orders, sems, order_sem
+    ) = refs[1 + CHIPS :]
     row_place, col_place = lax.axis_index("row"), lax.axis_index("col")
     chip = row_place // 2
+    pairs = [row_place * row_pairs + p for p in range(row_pairs)]
+    pairs += [col_place * col_pairs + p for p in range(col_pairs)]
+    heads = [
+        pltpu.make_async_copy(
+            index.at[1:2, pl.ds(pl.multiple_of(p * PAIR, PAIR), LL)],
+            orders.at[n : n + 1, :],
+            order_sem.at[n],
+        )
+        for n, p in enumerate(pairs)
+    ]
+    for head in heads:
+        head.start()
     copy = lambda s: pltpu.make_async_copy(
         cov.at[:, pl.ds(pl.multiple_of(s * STEP, STEP), STEP)], held.at[s], sems.at[s]
     )
     for s in range(steps):
         copy(s).start()
     legendre_table(by_degree, by_order)
+    for head in heads:
+        head.wait()
     row_w[...] = jnp.zeros_like(row_w)
     col_w[...] = jnp.zeros_like(col_w)
 
@@ -143,73 +158,107 @@
         return v
 
     for p in range(row_pairs):
-        first = orders[row_place * row_pairs + p]
-        for k, halves in enumerate(pair_weights(by_order, first, own_first)):
-            for h, v in enumerate(halves):
+        for k, sides in enumerate(pair_weights(by_order, orders[p, 0], own_first)):
+            for h, v in enumerate(sides):
                 if v is not None:
-                    row_w[2 * p + h, pl.ds(p * KEYS + k, NLAT, stride=row_pairs * KEYS), :] = v[
-                        :NLAT
-                    ]
-    for h in range(2 * row_pairs):
+                    row_w[
+                        p % GROUP * 2 + h, pl.ds(p * KEYS * NLAT + k, NLAT, stride=KEYS), :
+                    ] = v[:NLAT]
+    for h in range(2 * GROUP):
         row_wb[:, h * LL : (h + 1) * LL] = row_w[h].astype(BF16)
     for p in range(col_pairs):
-        first = orders[col_place * col_pairs + p]
         s, e = p // 2, p % 2
-        for k, halves in enumerate(pair_weights(by_order, first, lambda v: v)):
-            for h, v in enumerate(halves):
+        for k, sides in enumerate(
+            pair_weights(by_order, orders[row_pairs + p, 0], lambda v: v)
+        ):
+            for h, v in enumerate(sides):
                 if v is not None:
                     col_w[
-                        2 * e + h,
-                        pl.ds(s * NLAT * 2 * KEYS + e * KEYS + k, NLAT, stride=2 * KEYS),
-                        :,
+                        2 * e + h, pl.ds(s * LL + e * KEYS + k, NLAT, stride=2 * KEYS), :
                     ] = v[:NLAT]
-    for h in range(4):
-        high, low = split(col_w[h])
-        col_hi[:, h * LL : (h + 1) * LL] = high
-        col_lo[:, h * LL : (h + 1) * LL] = low
-
-    rows = NLAT * 2 * KEYS
-
-    def step(s, carry):
-        copy(s).wait()
-        first = jnp.dot(row_wb[...], held[s], preferred_element_type=F32)
-        own = pl.ds(pl.multiple_of(s * rows, rows), rows)
-        second = dot3((col_hi[own, :], col_lo[own, :]), split(first), ((1,), (1,)))
+    for s in range(steps):
+        for h in range(4):
+            high, low = split(col_w[h, s * LL : (s + 1) * LL, :].T)
+            col_wb[s, h * LL : (h + 1) * LL, :LL] = high
+            col_wb[s, h * LL : (h + 1) * LL, LL:] = low
+
+    def column_side(s, half):
+        both = lax.dot_general(
+            held[s], col_wb[s], (((1,), (0,)), ((), ())), preferred_element_type=F32
+        )
+        high, low = split(both[:, :LL] + both[:, LL:])
+        half[:, :LL] = high
+        half[:, LL:] = low
+
+    def row_side(s, half):
+        rows = GROUP * KEYS * NLAT
+        for q in range(row_pairs // GROUP):
+            both = jnp.dot(
+                row_wb[q * rows : (q + 1) * rows, :],
+                half[q * GROUP * PAIR : (q + 1) * GROUP * PAIR, :],
+                preferred_element_type=F32,
+            )
+            both = both[:, :LL] + both[:, LL:]
+            for g in range(GROUP):
+                for i in range(NLAT):
+                    row = (i * row_pairs + q * GROUP + g) * KEYS
+                    from_row = (g * NLAT + i) * KEYS
+                    second[row : row + KEYS, :] = both[from_row : from_row + KEYS]
+        part = row_pairs * KEYS * NLAT
         for t in range(CHUNKS):
+            turned = second[t * LL : (t + 1) * LL, :].T
             for g in range(NLAT // 4):
-                parts = [
-                    second[8 * (4 * g + u) : 8 * (4 * g + u + 1), LL * t : LL * (t + 1)]
-                    for u in range(4)
-                ]
-                for d, part in enumerate(turn4(parts)):
-                    outs[t * CHIPS + d][
-                        pl.ds(pl.multiple_of(s * 8, 8), 8), pl.ds(g * LL, LL)
-                    ] = part
+                xs = [turned[8 * (4 * g + u) : 8 * (4 * g + u + 1)] for u in range(4)]
+                for d, x in enumerate(turn4(xs)):
+                    lanes = slice(g * LL, (g + 1) * LL)
+                    if t == 0:
+                        lanes = slice(d * part + g * LL, d * part + (g + 1) * LL)
+                        first_out[pl.ds(pl.multiple_of(s * 8, 8), 8), lanes] = x
+                    else:
+                        row = (t - 1) * steps * 8 + s * 8
+                        later_outs[d][pl.ds(pl.multiple_of(row, 8), 8), lanes] = x
+
+    def both_sides(s, now, later):
+        copy(s + 1).wait()
+        column_side(s + 1, later)
+        row_side(s, now)
+
+    def step(j, carry):
+        both_sides(2 * j, even, odd)
+        both_sides(2 * j + 1, odd, even)
         return carry
 
-    lax.fori_loop(0, steps, step, 0)
-
-
-def order_sums(covariance, orders):
+    copy(0).wait()
+    column_side(0, even)
+    lax.fori_loop(0, steps // 2 - 1, step, 0)
+    both_sides(steps - 2, even, odd)
+    row_side(steps - 1, odd)
+
+
+def order_sums(covariance, coef_index):
     rows_dev, cols_dev = covariance.shape
     row_pairs, col_pairs, steps = rows_dev // PAIR, cols_dev // PAIR, cols_dev // STEP
-    lanes = NLAT * row_pairs * KEYS
-    out = jax.ShapeDtypeStruct((col_pairs * KEYS, lanes), F32)
+    lanes, keys = NLAT * row_pairs * KEYS, col_pairs * KEYS
+    later = jax.ShapeDtypeStruct(((CHUNKS - 1) * keys, lanes), F32)
     return pl.pallas_call(
         functools.partial(order_sums_kernel, row_pairs, col_pairs, steps),
-        out_shape=[out] * (CHUNKS * CHIPS),
-        in_specs=[pl.BlockSpec(memory_space=pltpu.SMEM), pl.BlockSpec(memory_space=pl.ANY)],
-        out_specs=[pl.BlockSpec(memory_space=pltpu.VMEM)] * (CHUNKS * CHIPS),
+        out_shape=[jax.ShapeDtypeStruct((keys, CHIPS * lanes), F32)] + [later] * CHIPS,
+        in_specs=[pl.BlockSpec(memory_space=pl.ANY)] * 2,
+        out_specs=[pl.BlockSpec(memory_space=pltpu.VMEM)] * (1 + CHIPS),
         scratch_shapes=[
             pltpu.VMEM((steps, rows_dev, STEP), BF16),
             pltpu.VMEM((LL * ROWS16, LL), F32),
             pltpu.VMEM((LL * ROWS16, LL), F32),
-            pltpu.VMEM((rows_dev // LL, lanes, LL), F32),
-            pltpu.VMEM((lanes, rows_dev), BF16),
-            pltpu.VMEM((STEP // LL, steps * NLAT * 2 * KEYS, LL), F32),
-            pltpu.VMEM((steps * NLAT * 2 * KEYS, STEP), BF16),
-            pltpu.VMEM((steps * NLAT * 2 * KEYS, STEP), BF16),
+            pltpu.VMEM((2 * GROUP, lanes, LL), F32),
+            pltpu.VMEM((lanes, GROUP * PAIR), BF16),
+            pltpu.VMEM((STEP // LL, steps * LL, LL), F32),
+            pltpu.VMEM((steps, STEP, 2 * LL), BF16),
+            pltpu.VMEM((rows_dev, 2 * LL), BF16),
+            pltpu.VMEM((rows_dev, 2 * LL), BF16),
+            pltpu.VMEM((lanes, LL), F32),
+            pltpu.SMEM((row_pairs + col_pairs, LL), jnp.int32),
             pltpu.SemaphoreType.DMA((steps,)),
+            pltpu.SemaphoreType.DMA((row_pairs + col_pairs,)),
         ],
         compiler_params=pltpu.CompilerParams(vmem_limit_bytes=56 * 1024 * 1024),
         cost_estimate=pl.CostEstimate(
@@ -218,7 +267,7 @@
             transcendentals=0,
         ),
         name="order_sums",
-    )(orders, covariance)
+    )(coef_index, covariance)
 
 
 def columns_kernel(own, near, outer, far, table, result, partial, rhs):
@@ -341,29 +390,60 @@
     return col_table, wave(row_lons, row_keys)
 
 
+def after(x, *done):
+    return lax.optimization_barrier((x, *done))[0]
+
+
 def chunked(covariance, coef_index):
-    orders = coef_index[1].reshape(-1, PAIR)[:, 0]
-    sums = order_sums(covariance, orders)
-    orders, *sums = lax.optimization_barrier((orders, *sums))
-    col_table, row_table = tables(orders)
     flip = lambda x, bits: lax.ppermute(
         x, "row", [(r, r ^ bits) for r in range(lax.axis_size("row"))]
     )
     along = lambda x, *pairs: lax.ppermute(x, "col", pairs)
-    parts = []
-    for t in range(CHUNKS):
-        mine = sums[t * CHIPS : (t + 1) * CHIPS]
-        own = jnp.concatenate(
-            [mine[0]] + [flip(mine[d], 2 * d) for d in range(1, CHIPS)], axis=1
-        )
-        near = along(own, (1, 2), (2, 1))
+
+    def spread(xs):
+        return [xs[0]] + [flip(xs[d], 2 * d) for d in range(1, CHIPS)]
+
+    def inward(own):
         outer = along(own, (0, 1), (3, 2))
-        far = along(outer, (1, 2), (2, 1))
-        result, partial = columns(own, near, outer, far, col_table)
-        result = result + along(partial, (1, 0), (2, 3))
-        grid = rows(result, flip(result, 1), row_table)
-        parts += [grid[0]] + [flip(grid[d], 2 * d) for d in range(1, CHIPS)]
-    return place(parts)
+        return along(own, (1, 2), (2, 1)), outer
+
+    def across(outer):
+        return along(outer, (1, 2), (2, 1))
+
+    def outward(result, partial):
+        return result + along(partial, (1, 0), (2, 3))
+
+    def finish(result):
+        return spread(rows(result, flip(result, 1), row_table))
+
+    own0, *later = order_sums(covariance, coef_index)
+    orders = after(coef_index, own0)[1].reshape(-1, PAIR)[:, 0]
+    col_table, row_table = tables(orders)
+    near0, outer0 = inward(own0)
+    later = spread(later)
+    far0 = across(outer0)
+    keys = own0.shape[0]
+    own1, own2 = (
+        jnp.concatenate([x[t * keys : (t + 1) * keys] for x in later], axis=1) for t in range(2)
+    )
+    near1, outer1 = inward(after(own1, near0, outer0))
+    result0, partial0 = columns(own0, near0, outer0, far0, col_table)
+    far1 = across(after(outer1, far0))
+    near2, outer2 = inward(after(own2, near1, outer1, partial0))
+    result0 = outward(result0, partial0)
+    result1, partial1 = columns(own1, near1, outer1, far1, col_table)
+    far2 = across(after(outer2, result0, partial1))
+    lanes = result0.shape[1] // CHIPS
+    result0 = jnp.concatenate(
+        spread([result0[:, d * lanes : (d + 1) * lanes] for d in range(CHIPS)]), axis=1
+    )
+    result2, partial2 = columns(own2, near2, outer2, far2, after(col_table, result0))
+    result1 = outward(result1, partial1)
+    grid0 = finish(result0)
+    result2 = outward(result2, after(partial2, result1))
+    grid1 = finish(result1)
+    grid2 = finish(after(result2, *grid0))
+    return place(grid0 + grid1 + grid2)
 
 
 def legendre_rows(lat_count, lon_count, degree_count):

time: 144 us -> 121 us (0.84)
  waiting for transfers between devices: 64.9 us -> 36.3 us
  starting transfers between devices: 43.1 us -> 54 us
  Pallas kernels: 25.5 us -> 21.8 us
    ppermute x12, waiting for transfers between devices: 47.4 us -> 15.4 us  [chunked(): along = lambda x, *pairs: lax.ppermute(x, 'col', pairs)]
    ppermute x12, starting transfers between devices: 18.4 us -> 34.1 us  [chunked(): along = lambda x, *pairs: lax.ppermute(x, 'col', pairs)]
    ppermute x21 -> x18, starting transfers between devices: 24.6 us -> 19.9 us  [chunked(): lax.ppermute(x, 'row', [(r, r ^ bits) for r in range(lax.axis_size('row'))])]
    pallas_call x1, Pallas kernels: 17.7 us -> 13.9 us  [order_sums(): pl.pallas_call(functools.partial(order_sums_kernel, row_pairs, col_pairs,...]
    ppermute x21 -> x18, waiting for transfers between devices: 17.6 us -> 20.8 us  [chunked(): lax.ppermute(x, 'row', [(r, r ^ bits) for r in range(lax.axis_size('row'))])]
    unnamed x12 -> x3, local copies, waits for them, and re-layouts: 3.35 us -> 1.06 us
    add x3, other arithmetic: 2.33 us -> 0.22 us  [outward(): return result + along(partial, (1, 0), (2, 3))]
    slice x2 -> x7, local copies, waits for them, and re-layouts: 1.14 us -> 2.84 us  [the longest x2 1.14 us: chunked(): orders = after(coef_index, own0)[1].reshape(-1, PAIR)[:, 0]]
  transfers between devices with their start and end apart: 33 -> 30, of which waited for: 12 -> 11; matrix products, arithmetic and copies ran while one was open for 5% -> 5% of each run, Pallas kernels for 4% -> 5%
where the time goes in v2:
time: 121 us; the launch traced here: 120 us
  starting transfers between devices  54 us (45%)
  waiting for transfers between devices  36.3 us (30%)
  Pallas kernels  21.8 us (18%)
  local copies, waits for them, and re-layouts  4.31 us (4%)
  other arithmetic  3.22 us (3%)
    ppermute x12, starting transfers between devices, chunked(): along = lambda x, *pairs: lax.ppermute(x, 'col', pairs)  34.1 us
    ppermute x18, waiting for transfers between devices, chunked(): lax.ppermute(x, 'row', [(r, r ^ bits) for r in range(lax.axis_size('row'))])  20.8 us
    ppermute x18, starting transfers between devices, chunked(): lax.ppermute(x, 'row', [(r, r ^ bits) for r in range(lax.axis_size('row'))])  19.9 us
    ppermute x12, waiting for transfers between devices, chunked(): along = lambda x, *pairs: lax.ppermute(x, 'col', pairs)  15.4 us
    pallas_call x1, Pallas kernels, order_sums(): pl.pallas_call(functools.partial(order_sums_kernel, row_pairs, col_pairs,...  13.9 us
    pallas_call x3, Pallas kernels, rows(): pl.pallas_call(rows_kernel, out_shape=[out] * CHIPS, in_specs=[pl.BlockSp...  3.91 us
  transfers between devices with their start and end apart: 30, of which 11 were waited for; matrix products, arithmetic and copies ran while one was open for 5% of the time, Pallas kernels for 5%

profile of v2, /device:TPU:0, one launch (start us, length us, event | category | flops | bytes accessed | tf_op | source)
XLA Modules:
  0.0 120.0 jit_solution(9866975153590181901)
XLA Ops:
  0.0 13.9 %order_sums.1 = (f32[64,1536]{1,0:T(8,128)}, f32[128,384]{1,0:T(8,128)}, f32[128,384]{1,0:T(8,128)}, f32[128,384]{1,0:T(8,128)}, f32[128,384]{1,0:T(8,128)}) custom-call(s32[3,16384]{1,0:T(4,128)} %index.1, bf16[2048,4096]{1,0:T(8,128)(2,1)} %cov.1), custom_call_target="tpu_custom_call" | custom-call | flops 6442450944 | bytes 16777216 | tf_op jit(solution)/shard_map/order_sums/pallas_call | solution.py:243
  13.9 5.0 %collective-permute-start.1 = (f32[64,1536]{1,0:T(8,128)}, f32[64,1536]{1,0:T(8,128)S(1)}, u32[]{:S(2)}, u32[]{:S(2)}) collective-permute-start(f32[64,1536]{1,0:T(8,128)} %get-tuple-element.36.own), channel_id=1, source_target_pairs={{0,1},{3,2},{4,5},{7,6},{8,9},{11,10},{12,13},{15,14},{16,17},{19,... | collective-permute-start | bytes 1179656 | tf_op jit(solution)/shard_map/ppermute | solution.py:401
  19.5 1.6 %collective-permute-start.11 = (f32[128,384]{1,0:T(8,128)}, f32[128,384]{1,0:T(8,128)S(1)}, u32[]{:S(2)}, u32[]{:S(2)}) collective-permute-start(f32[128,384]{1,0:T(8,128)} %get-tuple-element.45), channel_id=1, source_target_pairs={{0,8},{4,12},{8,0},{12,4},{16,24},{20,28},{24,16},{28,20},{1,9},{5... | collective-permute-start | bytes 589832 | tf_op jit(solution)/shard_map/ppermute | solution.py:398
  21.1 1.5 %collective-permute-start.12 = (f32[128,384]{1,0:T(8,128)}, f32[128,384]{1,0:T(8,128)S(1)}, u32[]{:S(2)}, u32[]{:S(2)}) collective-permute-start(f32[128,384]{1,0:T(8,128)} %get-tuple-element.46), channel_id=1, source_target_pairs={{0,16},{4,20},{8,24},{12,28},{16,0},{20,4},{24,8},{28,12},{1,17},{... | collective-permute-start | bytes 589832 | tf_op jit(solution)/shard_map/ppermute | solution.py:398
  27.7 3.9 %collective-permute-done.12 = f32[128,384]{1,0:T(8,128)S(1)} collective-permute-done((f32[128,384]{1,0:T(8,128)}, f32[128,384]{1,0:T(8,128)S(1)}, u32[]{:S(2)}, u32[]{:S(2)}) %collective-permute-start.12) | collective-permute-done | bytes 196640 | tf_op jit(solution)/shard_map/ppermute | solution.py:398
  32.4 5.8 %collective-permute-start.15 = (f32[64,1536]{1,0:T(8,128)S(1)}, f32[64,1536]{1,0:T(8,128)S(1)}, u32[]{:S(2)}, u32[]{:S(2)}) collective-permute-start(f32[64,1536]{1,0:T(8,128)S(1)} %pad_maximum_fusion.1.own), channel_id=1, source_target_pairs={{0,1},{3,2},{4,5},{7,6},{8,9},{11,10},{12,13},{15,14},{16,17},{19,... | collective-permute-start | bytes 1179656 | tf_op jit(solution)/shard_map/ppermute | solution.py:401
  41.8 1.6 %collective-permute-done.15.outer = f32[64,1536]{1,0:T(8,128)S(1)} collective-permute-done((f32[64,1536]{1,0:T(8,128)S(1)}, f32[64,1536]{1,0:T(8,128)S(1)}, u32[]{:S(2)}, u32[]{:S(2)}) %collective-permute-start.15) | collective-permute-done | bytes 393248 | tf_op jit(solution)/shard_map/ppermute | solution.py:401
  44.2 15.2 %collective-permute-start.23 = (f32[64,1536]{1,0:T(8,128)S(1)}, f32[64,1536]{1,0:T(8,128)S(1)}, u32[]{:S(2)}, u32[]{:S(2)}) collective-permute-start(f32[64,1536]{1,0:T(8,128)S(1)} %pad_maximum_fusion.2.own), channel_id=1, source_target_pairs={{0,1},{3,2},{4,5},{7,6},{8,9},{11,10},{12,13},{15,14},{16,17},{19,... | collective-permute-start | bytes 1179656 | tf_op jit(solution)/shard_map/ppermute | solution.py:401
  60.2 2.7 %collective-permute-start.4 = (f32[96,384]{1,0:T(8,128)}, f32[96,384]{1,0:T(8,128)S(1)}, u32[]{:S(2)}, u32[]{:S(2)}) collective-permute-start(f32[96,384]{1,0:T(8,128)} %get-tuple-element.74), channel_id=1, source_target_pairs={{0,8},{4,12},{8,0},{12,4},{16,24},{20,28},{24,16},{28,20},{1,9},{5... | collective-permute-start | bytes 442376 | tf_op jit(solution)/shard_map/ppermute | solution.py:398
  68.0 1.7 %collective-permute-done.6 = f32[96,384]{1,0:T(8,128)} collective-permute-done((f32[96,384]{1,0:T(8,128)S(1)}, f32[96,384]{1,0:T(8,128)}, u32[]{:S(2)}, u32[]{:S(2)}) %collective-permute-start.6) | collective-permute-done | bytes 147488 | tf_op jit(solution)/shard_map/ppermute | solution.py:398
  70.8 5.9 %collective-permute-done.17 = f32[96,1536]{1,0:T(8,128)S(1)} collective-permute-done((f32[96,1536]{1,0:T(8,128)S(1)}, f32[96,1536]{1,0:T(8,128)S(1)}, u32[]{:S(2)}, u32[]{:S(2)}) %collective-permute-start.17) | collective-permute-done | bytes 589856 | tf_op jit(solution)/shard_map/ppermute | solution.py:401
  77.5 1.5 %collective-permute-start.25 = (f32[96,1536]{1,0:T(8,128)S(1)}, f32[96,1536]{1,0:T(8,128)S(1)}, u32[]{:S(2)}, u32[]{:S(2)}) collective-permute-start(f32[96,1536]{1,0:T(8,128)S(1)} %get-tuple-element.61), channel_id=1, source_target_pairs={{1,0},{2,3},{5,4},{6,7},{9,8},{10,11},{13,12},{14,15},{17,16},{18,... | collective-permute-start | bytes 1769480 | tf_op jit(solution)/shard_map/ppermute | solution.py:401
  79.9 1.3 %rows.3 = (f32[48,1152]{1,0:T(8,128)S(1)}, f32[48,1152]{1,0:T(8,128)S(1)}, f32[48,1152]{1,0:T(8,128)S(1)}, f32[48,1152]{1,0:T(8,128)S(1)}) custom-call(f32[96,1536]{1,0:T(8,128)S(1)} %pad_maximum_fusion.mine, f32[96,1536]{1,0:T(8,128)S(1)} %collective-permute-done.7.other, f32[192,256]{1,0:T(8,128)S(1)} %fusion.6.table), custom_call_target="tpu_custom_call" | custom-call | flops 339738624 | bytes 2359296 | tf_op jit(solution)/shard_map/rows/pallas_call | solution.py:320
  81.2 2.3 %collective-permute-start.10 = (f32[48,1152]{1,0:T(8,128)S(1)}, f32[48,1152]{1,0:T(8,128)S(1)}, u32[]{:S(2)}, u32[]{:S(2)}) collective-permute-start(f32[48,1152]{1,0:T(8,128)S(1)} %get-tuple-element.43), channel_id=1, source_target_pairs={{0,24},{4,28},{8,16},{12,20},{16,8},{20,12},{24,0},{28,4},{1,25},{... | collective-permute-start | bytes 663560 | tf_op jit(solution)/shard_map/ppermute | solution.py:398
  84.8 7.9 %collective-permute-done.25 = f32[96,1536]{1,0:T(8,128)S(1)} collective-permute-done((f32[96,1536]{1,0:T(8,128)S(1)}, f32[96,1536]{1,0:T(8,128)S(1)}, u32[]{:S(2)}, u32[]{:S(2)}) %collective-permute-start.25) | collective-permute-done | bytes 589856 | tf_op jit(solution)/shard_map/ppermute | solution.py:401
  92.8 1.3 %rows.4 = (f32[48,1152]{1,0:T(8,128)S(1)}, f32[48,1152]{1,0:T(8,128)S(1)}, f32[48,1152]{1,0:T(8,128)S(1)}, f32[48,1152]{1,0:T(8,128)S(1)}) custom-call(f32[96,1536]{1,0:T(8,128)S(1)} %add.185.mine, f32[96,1536]{1,0:T(8,128)S(1)} %collective-permute-done.18.other, f32[192,256]{1,0:T(8,128)S(1)} %fusion.6.table), custom_call_target="tpu_custom_call" | custom-call | flops 339738624 | bytes 2359296 | tf_op jit(solution)/shard_map/rows/pallas_call | solution.py:320
  94.1 2.1 %collective-permute-start.19 = (f32[48,1152]{1,0:T(8,128)S(1)}, f32[48,1152]{1,0:T(8,128)S(1)}, u32[]{:S(2)}, u32[]{:S(2)}) collective-permute-start(f32[48,1152]{1,0:T(8,128)S(1)} %get-tuple-element.53), channel_id=1, source_target_pairs={{0,8},{4,12},{8,0},{12,4},{16,24},{20,28},{24,16},{28,20},{1,9},{5... | collective-permute-start | bytes 663560 | tf_op jit(solution)/shard_map/ppermute | solution.py:398
  97.8 1.3 %rows.5 = (f32[48,1152]{1,0:T(8,128)S(1)}, f32[48,1152]{1,0:T(8,128)S(1)}, f32[48,1152]{1,0:T(8,128)S(1)}, f32[48,1152]{1,0:T(8,128)S(1)}) custom-call(f32[96,1536]{1,0:T(8,128)S(1)} %add.186.mine, f32[96,1536]{1,0:T(8,128)S(1)} %collective-permute-done.26.other, f32[192,256]{1,0:T(8,128)S(1)} %fusion.6.table), custom_call_target="tpu_custom_call" | custom-call | flops 339738624 | bytes 2359296 | tf_op jit(solution)/shard_map/rows/pallas_call | solution.py:320
  99.1 2.0 %collective-permute-start.27 = (f32[48,1152]{1,0:T(8,128)S(1)}, f32[48,1152]{1,0:T(8,128)S(1)}, u32[]{:S(2)}, u32[]{:S(2)}) collective-permute-start(f32[48,1152]{1,0:T(8,128)S(1)} %get-tuple-element.64), channel_id=1, source_target_pairs={{0,8},{4,12},{8,0},{12,4},{16,24},{20,28},{24,16},{28,20},{1,9},{5... | collective-permute-start | bytes 663560 | tf_op jit(solution)/shard_map/ppermute | solution.py:398
  102.5 2.1 %collective-permute-start.29 = (f32[48,1152]{1,0:T(8,128)S(1)}, f32[48,1152]{1,0:T(8,128)S(1)}, u32[]{:S(2)}, u32[]{:S(2)}) collective-permute-start(f32[48,1152]{1,0:T(8,128)S(1)} %get-tuple-element.66), channel_id=1, source_target_pairs={{0,24},{4,28},{8,16},{12,20},{16,8},{20,12},{24,0},{28,4},{1,25},{... | collective-permute-start | bytes 663560 | tf_op jit(solution)/shard_map/ppermute | solution.py:398
  104.6 4.6 %collective-permute-done.20.refs_6_ = f32[48,1152]{1,0:T(8,128)S(1)} collective-permute-done((f32[48,1152]{1,0:T(8,128)S(1)}, f32[48,1152]{1,0:T(8,128)S(1)}, u32[]{:S(2)}, u32[]{:S(2)}) %collective-permute-start.20) | collective-permute-done | bytes 221216 | tf_op jit(solution)/shard_map/ppermute | solution.py:398
  109.2 2.8 %collective-permute-done.27.refs_9_ = f32[48,1152]{1,0:T(8,128)S(1)} collective-permute-done((f32[48,1152]{1,0:T(8,128)S(1)}, f32[48,1152]{1,0:T(8,128)S(1)}, u32[]{:S(2)}, u32[]{:S(2)}) %collective-permute-start.27) | collective-permute-done | bytes 221216 | tf_op jit(solution)/shard_map/ppermute | solution.py:398
  112.0 6.0 %collective-permute-done.28.refs_10_ = f32[48,1152]{1,0:T(8,128)S(1)} collective-permute-done((f32[48,1152]{1,0:T(8,128)S(1)}, f32[48,1152]{1,0:T(8,128)S(1)}, u32[]{:S(2)}, u32[]{:S(2)}) %collective-permute-start.28) | collective-permute-done | bytes 221216 | tf_op jit(solution)/shard_map/ppermute | solution.py:398
  118.0 2.1 %place.1 = f32[576,1152]{1,0:T(8,128)} custom-call(f32[48,1152]{1,0:T(8,128)S(1)} %get-tuple-element.40.refs_0_, f32[48,1152]{1,0:T(8,128)S(1)} %collective-permute-done.8.refs_1_, f32[48,1152]{1,0:T(8,128)S(1)} %collective-permute-done.9.refs_2_, f32[48,1152]{1,0:T(8,128)S(1)} %collective-permute-done.10.refs_3_, f32[48,1152]{1,0:T(8,128)S(1)} %get-tuple-element.52.refs_4_, ...), custom_call_target="tpu_custom_call" | custom-call | tf_op jit(solution)/shard_map/place/pallas_call | solution.py:350
  (80 shorter events, 23.6 us)
Async XLA Ops:
  13.9 17.7 %collective-permute-start.1 = (f32[64,1536]{1,0:T(8,128)}, f32[64,1536]{1,0:T(8,128)S(1)}, u32[]{:S(2)}, u32[]{:S(2)}) collective-permute-start(f32[64,1536]{1,0:T(8,128)} %get-tuple-element.36.own), channel_id=1, source_target_pairs={{0,1},{3,2},{4,5},{7,6},{8,9},{11,10},{12,13},{15,14},{16,17},{19,... | collective-permute-start | bytes 1179656 | tf_op jit(solution)/shard_map/ppermute | solution.py:401
  18.9 13.6 %collective-permute-start = (f32[64,1536]{1,0:T(8,128)}, f32[64,1536]{1,0:T(8,128)S(1)}, u32[]{:S(2)}, u32[]{:S(2)}) collective-permute-start(f32[64,1536]{1,0:T(8,128)} %get-tuple-element.36.own), channel_id=1, source_target_pairs={{1,2},{2,1},{5,6},{6,5},{9,10},{10,9},{13,14},{14,13},{17,18},{18,... | collective-permute-start | bytes 1179656 | tf_op jit(solution)/shard_map/ppermute | solution.py:401
  19.5 8.1 %collective-permute-start.11 = (f32[128,384]{1,0:T(8,128)}, f32[128,384]{1,0:T(8,128)S(1)}, u32[]{:S(2)}, u32[]{:S(2)}) collective-permute-start(f32[128,384]{1,0:T(8,128)} %get-tuple-element.45), channel_id=1, source_target_pairs={{0,8},{4,12},{8,0},{12,4},{16,24},{20,28},{24,16},{28,20},{1,9},{5... | collective-permute-start | bytes 589832 | tf_op jit(solution)/shard_map/ppermute | solution.py:398
  21.1 10.5 %collective-permute-start.12 = (f32[128,384]{1,0:T(8,128)}, f32[128,384]{1,0:T(8,128)S(1)}, u32[]{:S(2)}, u32[]{:S(2)}) collective-permute-start(f32[128,384]{1,0:T(8,128)} %get-tuple-element.46), channel_id=1, source_target_pairs={{0,16},{4,20},{8,24},{12,28},{16,0},{20,4},{24,8},{28,12},{1,17},{... | collective-permute-start | bytes 589832 | tf_op jit(solution)/shard_map/ppermute | solution.py:398
  22.6 9.7 %collective-permute-start.13 = (f32[128,384]{1,0:T(8,128)}, f32[128,384]{1,0:T(8,128)S(1)}, u32[]{:S(2)}, u32[]{:S(2)}) collective-permute-start(f32[128,384]{1,0:T(8,128)} %get-tuple-element.47), channel_id=1, source_target_pairs={{0,24},{4,28},{8,16},{12,20},{16,8},{20,12},{24,0},{28,4},{1,25},{... | collective-permute-start | bytes 589832 | tf_op jit(solution)/shard_map/ppermute | solution.py:398
  32.4 11.0 %collective-permute-start.15 = (f32[64,1536]{1,0:T(8,128)S(1)}, f32[64,1536]{1,0:T(8,128)S(1)}, u32[]{:S(2)}, u32[]{:S(2)}) collective-permute-start(f32[64,1536]{1,0:T(8,128)S(1)} %pad_maximum_fusion.1.own), channel_id=1, source_target_pairs={{0,1},{3,2},{4,5},{7,6},{8,9},{11,10},{12,13},{15,14},{16,17},{19,... | collective-permute-start | bytes 1179656 | tf_op jit(solution)/shard_map/ppermute | solution.py:401
  39.8 19.5 %collective-permute-start.3 = (f32[96,1536]{1,0:T(8,128)S(1)}, f32[96,1536]{1,0:T(8,128)S(1)}, u32[]{:S(2)}, u32[]{:S(2)}) collective-permute-start(f32[96,1536]{1,0:T(8,128)S(1)} %get-tuple-element.39), channel_id=1, source_target_pairs={{1,0},{2,3},{5,4},{6,7},{9,8},{10,11},{13,12},{14,15},{17,16},{18,... | collective-permute-start | bytes 1769480 | tf_op jit(solution)/shard_map/ppermute | solution.py:401
  43.4 20.9 %collective-permute-start.16 = (f32[64,1536]{1,0:T(8,128)S(1)}, f32[64,1536]{1,0:T(8,128)S(1)}, u32[]{:S(2)}, u32[]{:S(2)}) collective-permute-start(f32[64,1536]{1,0:T(8,128)S(1)} %collective-permute-done.15.outer), channel_id=1, source_target_pairs={{1,2},{2,1},{5,6},{6,5},{9,10},{10,9},{13,14},{14,13},{17,18},{18,... | collective-permute-start | bytes 1179656 | tf_op jit(solution)/shard_map/ppermute | solution.py:401
  44.2 22.1 %collective-permute-start.23 = (f32[64,1536]{1,0:T(8,128)S(1)}, f32[64,1536]{1,0:T(8,128)S(1)}, u32[]{:S(2)}, u32[]{:S(2)}) collective-permute-start(f32[64,1536]{1,0:T(8,128)S(1)} %pad_maximum_fusion.2.own), channel_id=1, source_target_pairs={{0,1},{3,2},{4,5},{7,6},{8,9},{11,10},{12,13},{15,14},{16,17},{19,... | collective-permute-start | bytes 1179656 | tf_op jit(solution)/shard_map/ppermute | solution.py:401
  65.0 11.8 %collective-permute-start.17 = (f32[96,1536]{1,0:T(8,128)S(1)}, f32[96,1536]{1,0:T(8,128)S(1)}, u32[]{:S(2)}, u32[]{:S(2)}) collective-permute-start(f32[96,1536]{1,0:T(8,128)S(1)} %get-tuple-element.51), channel_id=1, source_target_pairs={{1,0},{2,3},{5,4},{6,7},{9,8},{10,11},{13,12},{14,15},{17,16},{18,... | collective-permute-start | bytes 1769480 | tf_op jit(solution)/shard_map/ppermute | solution.py:401
  66.3 10.5 %collective-permute-start.22 = (f32[64,1536]{1,0:T(8,128)S(1)}, f32[64,1536]{1,0:T(8,128)S(1)}, u32[]{:S(2)}, u32[]{:S(2)}) collective-permute-start(f32[64,1536]{1,0:T(8,128)S(1)} %pad_maximum_fusion.2.own), channel_id=1, source_target_pairs={{1,2},{2,1},{5,6},{6,5},{9,10},{10,9},{13,14},{14,13},{17,18},{18,... | collective-permute-start | bytes 1179656 | tf_op jit(solution)/shard_map/ppermute | solution.py:401
  67.0 9.8 %collective-permute-start.24 = (f32[64,1536]{1,0:T(8,128)S(1)}, f32[64,1536]{1,0:T(8,128)S(1)}, u32[]{:S(2)}, u32[]{:S(2)}) collective-permute-start(f32[64,1536]{1,0:T(8,128)S(1)} %collective-permute-done.23.outer), channel_id=1, source_target_pairs={{1,2},{2,1},{5,6},{6,5},{9,10},{10,9},{13,14},{14,13},{17,18},{18,... | collective-permute-start | bytes 1179656 | tf_op jit(solution)/shard_map/ppermute | solution.py:401
  70.7 9.2 %collective-permute-start.7 = (f32[96,1536]{1,0:T(8,128)S(1)}, f32[96,1536]{1,0:T(8,128)S(1)}, u32[]{:S(2)}, u32[]{:S(2)}) collective-permute-start(f32[96,1536]{1,0:T(8,128)S(1)} %pad_maximum_fusion.mine), channel_id=1, source_target_pairs={{0,4},{4,0},{8,12},{12,8},{16,20},{20,16},{24,28},{28,24},{1,5},{5... | collective-permute-start | bytes 1769480 | tf_op jit(solution)/shard_map/ppermute | solution.py:398
  77.5 15.1 %collective-permute-start.25 = (f32[96,1536]{1,0:T(8,128)S(1)}, f32[96,1536]{1,0:T(8,128)S(1)}, u32[]{:S(2)}, u32[]{:S(2)}) collective-permute-start(f32[96,1536]{1,0:T(8,128)S(1)} %get-tuple-element.61), channel_id=1, source_target_pairs={{1,0},{2,3},{5,4},{6,7},{9,8},{10,11},{13,12},{14,15},{17,16},{18,... | collective-permute-start | bytes 1769480 | tf_op jit(solution)/shard_map/ppermute | solution.py:401
  81.2 11.5 %collective-permute-start.10 = (f32[48,1152]{1,0:T(8,128)S(1)}, f32[48,1152]{1,0:T(8,128)S(1)}, u32[]{:S(2)}, u32[]{:S(2)}) collective-permute-start(f32[48,1152]{1,0:T(8,128)S(1)} %get-tuple-element.43), channel_id=1, source_target_pairs={{0,24},{4,28},{8,16},{12,20},{16,8},{20,12},{24,0},{28,4},{1,25},{... | collective-permute-start | bytes 663560 | tf_op jit(solution)/shard_map/ppermute | solution.py:398
  83.5 9.3 %collective-permute-start.8 = (f32[48,1152]{1,0:T(8,128)S(1)}, f32[48,1152]{1,0:T(8,128)S(1)}, u32[]{:S(2)}, u32[]{:S(2)}) collective-permute-start(f32[48,1152]{1,0:T(8,128)S(1)} %get-tuple-element.41), channel_id=1, source_target_pairs={{0,8},{4,12},{8,0},{12,4},{16,24},{20,28},{24,16},{28,20},{1,9},{5... | collective-permute-start | bytes 663560 | tf_op jit(solution)/shard_map/ppermute | solution.py:398
  83.9 8.9 %collective-permute-start.9 = (f32[48,1152]{1,0:T(8,128)S(1)}, f32[48,1152]{1,0:T(8,128)S(1)}, u32[]{:S(2)}, u32[]{:S(2)}) collective-permute-start(f32[48,1152]{1,0:T(8,128)S(1)} %get-tuple-element.42), channel_id=1, source_target_pairs={{0,16},{4,20},{8,24},{12,28},{16,0},{20,4},{24,8},{28,12},{1,17},{... | collective-permute-start | bytes 663560 | tf_op jit(solution)/shard_map/ppermute | solution.py:398
  84.8 8.1 %collective-permute-start.18 = (f32[96,1536]{1,0:T(8,128)S(1)}, f32[96,1536]{1,0:T(8,128)S(1)}, u32[]{:S(2)}, u32[]{:S(2)}) collective-permute-start(f32[96,1536]{1,0:T(8,128)S(1)} %add.185.mine), channel_id=1, source_target_pairs={{0,4},{4,0},{8,12},{12,8},{16,20},{20,16},{24,28},{28,24},{1,5},{5... | collective-permute-start | bytes 1769480 | tf_op jit(solution)/shard_map/ppermute | solution.py:398
  94.1 8.4 %collective-permute-start.19 = (f32[48,1152]{1,0:T(8,128)S(1)}, f32[48,1152]{1,0:T(8,128)S(1)}, u32[]{:S(2)}, u32[]{:S(2)}) collective-permute-start(f32[48,1152]{1,0:T(8,128)S(1)} %get-tuple-element.53), channel_id=1, source_target_pairs={{0,8},{4,12},{8,0},{12,4},{16,24},{20,28},{24,16},{28,20},{1,9},{5... | collective-permute-start | bytes 663560 | tf_op jit(solution)/shard_map/ppermute | solution.py:398
  96.2 13.0 %collective-permute-start.20 = (f32[48,1152]{1,0:T(8,128)S(1)}, f32[48,1152]{1,0:T(8,128)S(1)}, u32[]{:S(2)}, u32[]{:S(2)}) collective-permute-start(f32[48,1152]{1,0:T(8,128)S(1)} %get-tuple-element.54), channel_id=1, source_target_pairs={{0,16},{4,20},{8,24},{12,28},{16,0},{20,4},{24,8},{28,12},{1,17},{... | collective-permute-start | bytes 663560 | tf_op jit(solution)/shard_map/ppermute | solution.py:398
  97.0 12.3 %collective-permute-start.21 = (f32[48,1152]{1,0:T(8,128)S(1)}, f32[48,1152]{1,0:T(8,128)S(1)}, u32[]{:S(2)}, u32[]{:S(2)}) collective-permute-start(f32[48,1152]{1,0:T(8,128)S(1)} %get-tuple-element.55), channel_id=1, source_target_pairs={{0,24},{4,28},{8,16},{12,20},{16,8},{20,12},{24,0},{28,4},{1,25},{... | collective-permute-start | bytes 663560 | tf_op jit(solution)/shard_map/ppermute | solution.py:398
  99.1 13.0 %collective-permute-start.27 = (f32[48,1152]{1,0:T(8,128)S(1)}, f32[48,1152]{1,0:T(8,128)S(1)}, u32[]{:S(2)}, u32[]{:S(2)}) collective-permute-start(f32[48,1152]{1,0:T(8,128)S(1)} %get-tuple-element.64), channel_id=1, source_target_pairs={{0,8},{4,12},{8,0},{12,4},{16,24},{20,28},{24,16},{28,20},{1,9},{5... | collective-permute-start | bytes 663560 | tf_op jit(solution)/shard_map/ppermute | solution.py:398
  101.1 16.9 %collective-permute-start.28 = (f32[48,1152]{1,0:T(8,128)S(1)}, f32[48,1152]{1,0:T(8,128)S(1)}, u32[]{:S(2)}, u32[]{:S(2)}) collective-permute-start(f32[48,1152]{1,0:T(8,128)S(1)} %get-tuple-element.65), channel_id=1, source_target_pairs={{0,16},{4,20},{8,24},{12,28},{16,0},{20,4},{24,8},{28,12},{1,17},{... | collective-permute-start | bytes 663560 | tf_op jit(solution)/shard_map/ppermute | solution.py:398
  102.5 15.5 %collective-permute-start.29 = (f32[48,1152]{1,0:T(8,128)S(1)}, f32[48,1152]{1,0:T(8,128)S(1)}, u32[]{:S(2)}, u32[]{:S(2)}) collective-permute-start(f32[48,1152]{1,0:T(8,128)S(1)} %get-tuple-element.66), channel_id=1, source_target_pairs={{0,24},{4,28},{8,16},{12,20},{16,8},{20,12},{24,0},{28,4},{1,25},{... | collective-permute-start | bytes 663560 | tf_op jit(solution)/shard_map/ppermute | solution.py:398
  (7 other events, 33.7 us)

commit v3 on v2

--- a/solution.py
+++ b/solution.py
@@ -182,28 +182,28 @@
             col_wb[s, h * LL : (h + 1) * LL, :LL] = high
             col_wb[s, h * LL : (h + 1) * LL, LL:] = low
 
-    def column_side(s, half):
-        both = lax.dot_general(
-            held[s], col_wb[s], (((1,), (0,)), ((), ())), preferred_element_type=F32
-        )
+    blocks = row_pairs // GROUP
+    own = lambda q: slice(q * GROUP * PAIR, (q + 1) * GROUP * PAIR)
+
+    def column_block(s, half, q):
+        both = jnp.dot(held[s, own(q), :], col_wb[s], preferred_element_type=F32)
         high, low = split(both[:, :LL] + both[:, LL:])
-        half[:, :LL] = high
-        half[:, LL:] = low
-
-    def row_side(s, half):
+        half[own(q), :LL] = high
+        half[own(q), LL:] = low
+
+    def row_block(half, q):
         rows = GROUP * KEYS * NLAT
-        for q in range(row_pairs // GROUP):
-            both = jnp.dot(
-                row_wb[q * rows : (q + 1) * rows, :],
-                half[q * GROUP * PAIR : (q + 1) * GROUP * PAIR, :],
-                preferred_element_type=F32,
-            )
-            both = both[:, :LL] + both[:, LL:]
-            for g in range(GROUP):
-                for i in range(NLAT):
-                    row = (i * row_pairs + q * GROUP + g) * KEYS
-                    from_row = (g * NLAT + i) * KEYS
-                    second[row : row + KEYS, :] = both[from_row : from_row + KEYS]
+        both = jnp.dot(
+            row_wb[q * rows : (q + 1) * rows, :], half[own(q), :], preferred_element_type=F32
+        )
+        both = both[:, :LL] + both[:, LL:]
+        for g in range(GROUP):
+            for i in range(NLAT):
+                row = (i * row_pairs + q * GROUP + g) * KEYS
+                from_row = (g * NLAT + i) * KEYS
+                second[row : row + KEYS, :] = both[from_row : from_row + KEYS]
+
+    def store(s):
         part = row_pairs * KEYS * NLAT
         for t in range(CHUNKS):
             turned = second[t * LL : (t + 1) * LL, :].T
@@ -220,8 +220,12 @@
 
     def both_sides(s, now, later):
         copy(s + 1).wait()
-        column_side(s + 1, later)
-        row_side(s, now)
+        for q in range(blocks):
+            row_block(now, q)
+        for q in range(blocks - 1):
+            column_block(s + 1, later, q)
+        store(s)
+        column_block(s + 1, later, blocks - 1)
 
     def step(j, carry):
         both_sides(2 * j, even, odd)
@@ -229,10 +233,13 @@
         return carry
 
     copy(0).wait()
-    column_side(0, even)
+    for q in range(blocks):
+        column_block(0, even, q)
     lax.fori_loop(0, steps // 2 - 1, step, 0)
     both_sides(steps - 2, even, odd)
-    row_side(steps - 1, odd)
+    for q in range(blocks):
+        row_block(odd, q)
+    store(steps - 1)
 
 
 def order_sums(covariance, coef_index):
@@ -429,7 +436,8 @@
     near1, outer1 = inward(after(own1, near0, outer0))
     result0, partial0 = columns(own0, near0, outer0, far0, col_table)
     far1 = across(after(outer1, far0))
-    near2, outer2 = inward(after(own2, near1, outer1, partial0))
+    near2 = along(after(own2, near1, partial0), (1, 2), (2, 1))
+    outer2 = along(after(own2, outer1, partial0), (0, 1), (3, 2))
     result0 = outward(result0, partial0)
     result1, partial1 = columns(own1, near1, outer1, far1, col_table)
     far2 = across(after(outer2, result0, partial1))

time: 121 us -> 118 us (0.975)
  starting transfers between devices: 54 us -> 50.5 us
  waiting for transfers between devices: 36.3 us -> 39.5 us
  Pallas kernels: 21.8 us -> 19.4 us
    ppermute x12, starting transfers between devices: 34.1 us -> 29 us  [chunked(): along = lambda x, *pairs: lax.ppermute(x, 'col', pairs)]
    pallas_call x1, Pallas kernels: 13.9 us -> 11.5 us  [order_sums(): pl.pallas_call(functools.partial(order_sums_kernel, row_pairs, col_pairs,...]
    ppermute x18, waiting for transfers between devices: 20.8 us -> 22.9 us  [chunked(): lax.ppermute(x, 'row', [(r, r ^ bits) for r in range(lax.axis_size('row'))])]
    ppermute x18, starting transfers between devices: 19.9 us -> 21.5 us  [chunked(): lax.ppermute(x, 'row', [(r, r ^ bits) for r in range(lax.axis_size('row'))])]
  transfers between devices with their start and end apart: 30 -> 30, of which waited for: 11 -> 10; matrix products, arithmetic and copies ran while one was open for 5% -> 6% of each run, Pallas kernels for 5% -> 5%
where the time goes in v3:
time: 118 us; the launch traced here: 117 us
  starting transfers between devices  50.5 us (43%)
  waiting for transfers between devices  39.5 us (33%)
  Pallas kernels  19.4 us (16%)
  local copies, waits for them, and re-layouts  4.31 us (4%)
  other arithmetic  3.22 us (3%)
    ppermute x12, starting transfers between devices, chunked(): along = lambda x, *pairs: lax.ppermute(x, 'col', pairs)  29 us
    ppermute x18, waiting for transfers between devices, chunked(): lax.ppermute(x, 'row', [(r, r ^ bits) for r in range(lax.axis_size('row'))])  22.9 us
    ppermute x18, starting transfers between devices, chunked(): lax.ppermute(x, 'row', [(r, r ^ bits) for r in range(lax.axis_size('row'))])  21.5 us
    ppermute x12, waiting for transfers between devices, chunked(): along = lambda x, *pairs: lax.ppermute(x, 'col', pairs)  16.6 us
    pallas_call x1, Pallas kernels, order_sums(): pl.pallas_call(functools.partial(order_sums_kernel, row_pairs, col_pairs,...  11.5 us
    pallas_call x3, Pallas kernels, rows(): pl.pallas_call(rows_kernel, out_shape=[out] * CHIPS, in_specs=[pl.BlockSp...  3.91 us
  transfers between devices with their start and end apart: 30, of which 10 were waited for; matrix products, arithmetic and copies ran while one was open for 6% of the time, Pallas kernels for 5%

profile of v3, /device:TPU:0, one launch (start us, length us, event | category | flops | bytes accessed | tf_op | source)
XLA Modules:
  0.0 117.4 jit_solution(2584830427061479985)
XLA Ops:
  0.0 11.5 %order_sums.1 = (f32[64,1536]{1,0:T(8,128)}, f32[128,384]{1,0:T(8,128)}, f32[128,384]{1,0:T(8,128)}, f32[128,384]{1,0:T(8,128)}, f32[128,384]{1,0:T(8,128)}) custom-call(s32[3,16384]{1,0:T(4,128)} %index.1, bf16[2048,4096]{1,0:T(8,128)(2,1)} %cov.1), custom_call_target="tpu_custom_call" | custom-call | flops 6442450944 | bytes 16777216 | tf_op jit(solution)/shard_map/order_sums/pallas_call | solution.py:250
  11.5 5.0 %collective-permute-start.1 = (f32[64,1536]{1,0:T(8,128)}, f32[64,1536]{1,0:T(8,128)S(1)}, u32[]{:S(2)}, u32[]{:S(2)}) collective-permute-start(f32[64,1536]{1,0:T(8,128)} %get-tuple-element.37.own), channel_id=1, source_target_pairs={{0,1},{3,2},{4,5},{7,6},{8,9},{11,10},{12,13},{15,14},{16,17},{19,... | collective-permute-start | bytes 1179656 | tf_op jit(solution)/shard_map/ppermute | solution.py:408
  17.1 1.6 %collective-permute-start.11 = (f32[128,384]{1,0:T(8,128)}, f32[128,384]{1,0:T(8,128)S(1)}, u32[]{:S(2)}, u32[]{:S(2)}) collective-permute-start(f32[128,384]{1,0:T(8,128)} %get-tuple-element.46), channel_id=1, source_target_pairs={{0,8},{4,12},{8,0},{12,4},{16,24},{20,28},{24,16},{28,20},{1,9},{5... | collective-permute-start | bytes 589832 | tf_op jit(solution)/shard_map/ppermute | solution.py:405
  18.7 1.5 %collective-permute-start.12 = (f32[128,384]{1,0:T(8,128)}, f32[128,384]{1,0:T(8,128)S(1)}, u32[]{:S(2)}, u32[]{:S(2)}) collective-permute-start(f32[128,384]{1,0:T(8,128)} %get-tuple-element.47), channel_id=1, source_target_pairs={{0,16},{4,20},{8,24},{12,28},{16,0},{20,4},{24,8},{28,12},{1,17},{... | collective-permute-start | bytes 589832 | tf_op jit(solution)/shard_map/ppermute | solution.py:405
  25.3 3.9 %collective-permute-done.12 = f32[128,384]{1,0:T(8,128)S(1)} collective-permute-done((f32[128,384]{1,0:T(8,128)}, f32[128,384]{1,0:T(8,128)S(1)}, u32[]{:S(2)}, u32[]{:S(2)}) %collective-permute-start.12) | collective-permute-done | bytes 196640 | tf_op jit(solution)/shard_map/ppermute | solution.py:405
  30.0 5.8 %collective-permute-start.15 = (f32[64,1536]{1,0:T(8,128)S(1)}, f32[64,1536]{1,0:T(8,128)S(1)}, u32[]{:S(2)}, u32[]{:S(2)}) collective-permute-start(f32[64,1536]{1,0:T(8,128)S(1)} %pad_maximum_fusion.1.own), channel_id=1, source_target_pairs={{0,1},{3,2},{4,5},{7,6},{8,9},{11,10},{12,13},{15,14},{16,17},{19,... | collective-permute-start | bytes 1179656 | tf_op jit(solution)/shard_map/ppermute | solution.py:408
  39.4 1.6 %collective-permute-done.15.outer = f32[64,1536]{1,0:T(8,128)S(1)} collective-permute-done((f32[64,1536]{1,0:T(8,128)S(1)}, f32[64,1536]{1,0:T(8,128)S(1)}, u32[]{:S(2)}, u32[]{:S(2)}) %collective-permute-start.15) | collective-permute-done | bytes 393248 | tf_op jit(solution)/shard_map/ppermute | solution.py:408
  41.8 10.1 %collective-permute-start.23 = (f32[64,1536]{1,0:T(8,128)S(1)}, f32[64,1536]{1,0:T(8,128)S(1)}, u32[]{:S(2)}, u32[]{:S(2)}) collective-permute-start(f32[64,1536]{1,0:T(8,128)S(1)} %pad_maximum_fusion.2.own), channel_id=1, source_target_pairs={{0,1},{3,2},{4,5},{7,6},{8,9},{11,10},{12,13},{15,14},{16,17},{19,... | collective-permute-start | bytes 1179656 | tf_op jit(solution)/shard_map/ppermute | solution.py:408
  52.7 1.4 %collective-permute-start.4 = (f32[96,384]{1,0:T(8,128)}, f32[96,384]{1,0:T(8,128)S(1)}, u32[]{:S(2)}, u32[]{:S(2)}) collective-permute-start(f32[96,384]{1,0:T(8,128)} %get-tuple-element.76), channel_id=1, source_target_pairs={{0,8},{4,12},{8,0},{12,4},{16,24},{20,28},{24,16},{28,20},{1,9},{5... | collective-permute-start | bytes 442376 | tf_op jit(solution)/shard_map/ppermute | solution.py:405
  59.5 1.7 %collective-permute-done.6 = f32[96,384]{1,0:T(8,128)} collective-permute-done((f32[96,384]{1,0:T(8,128)S(1)}, f32[96,384]{1,0:T(8,128)}, u32[]{:S(2)}, u32[]{:S(2)}) %collective-permute-start.6) | collective-permute-done | bytes 147488 | tf_op jit(solution)/shard_map/ppermute | solution.py:405
  62.4 6.7 %collective-permute-done.17 = f32[96,1536]{1,0:T(8,128)S(1)} collective-permute-done((f32[96,1536]{1,0:T(8,128)S(1)}, f32[96,1536]{1,0:T(8,128)S(1)}, u32[]{:S(2)}, u32[]{:S(2)}) %collective-permute-start.17) | collective-permute-done | bytes 589856 | tf_op jit(solution)/shard_map/ppermute | solution.py:408
  69.8 1.5 %collective-permute-start.25 = (f32[96,1536]{1,0:T(8,128)S(1)}, f32[96,1536]{1,0:T(8,128)S(1)}, u32[]{:S(2)}, u32[]{:S(2)}) collective-permute-start(f32[96,1536]{1,0:T(8,128)S(1)} %get-tuple-element.63), channel_id=1, source_target_pairs={{1,0},{2,3},{5,4},{6,7},{9,8},{10,11},{13,12},{14,15},{17,16},{18,... | collective-permute-start | bytes 1769480 | tf_op jit(solution)/shard_map/ppermute | solution.py:408
  73.5 3.1 %collective-permute-start.10 = (f32[48,1152]{1,0:T(8,128)S(1)}, f32[48,1152]{1,0:T(8,128)S(1)}, u32[]{:S(2)}, u32[]{:S(2)}) collective-permute-start(f32[48,1152]{1,0:T(8,128)S(1)} %get-tuple-element.44), channel_id=1, source_target_pairs={{0,24},{4,28},{8,16},{12,20},{16,8},{20,12},{24,0},{28,4},{1,25},{... | collective-permute-start | bytes 663560 | tf_op jit(solution)/shard_map/ppermute | solution.py:405
  76.6 1.4 %collective-permute-start.8 = (f32[48,1152]{1,0:T(8,128)S(1)}, f32[48,1152]{1,0:T(8,128)S(1)}, u32[]{:S(2)}, u32[]{:S(2)}) collective-permute-start(f32[48,1152]{1,0:T(8,128)S(1)} %get-tuple-element.42), channel_id=1, source_target_pairs={{0,8},{4,12},{8,0},{12,4},{16,24},{20,28},{24,16},{28,20},{1,9},{5... | collective-permute-start | bytes 663560 | tf_op jit(solution)/shard_map/ppermute | solution.py:405
  77.9 1.4 %collective-permute-start.9 = (f32[48,1152]{1,0:T(8,128)S(1)}, f32[48,1152]{1,0:T(8,128)S(1)}, u32[]{:S(2)}, u32[]{:S(2)}) collective-permute-start(f32[48,1152]{1,0:T(8,128)S(1)} %get-tuple-element.43), channel_id=1, source_target_pairs={{0,16},{4,20},{8,24},{12,28},{16,0},{20,4},{24,8},{28,12},{1,17},{... | collective-permute-start | bytes 663560 | tf_op jit(solution)/shard_map/ppermute | solution.py:405
  79.3 8.3 %collective-permute-done.25 = f32[96,1536]{1,0:T(8,128)S(1)} collective-permute-done((f32[96,1536]{1,0:T(8,128)S(1)}, f32[96,1536]{1,0:T(8,128)S(1)}, u32[]{:S(2)}, u32[]{:S(2)}) %collective-permute-start.25) | collective-permute-done | bytes 589856 | tf_op jit(solution)/shard_map/ppermute | solution.py:408
  89.1 4.4 %collective-permute-start.19 = (f32[48,1152]{1,0:T(8,128)S(1)}, f32[48,1152]{1,0:T(8,128)S(1)}, u32[]{:S(2)}, u32[]{:S(2)}) collective-permute-start(f32[48,1152]{1,0:T(8,128)S(1)} %get-tuple-element.54), channel_id=1, source_target_pairs={{0,8},{4,12},{8,0},{12,4},{16,24},{20,28},{24,16},{28,20},{1,9},{5... | collective-permute-start | bytes 663560 | tf_op jit(solution)/shard_map/ppermute | solution.py:405
  93.6 1.5 %collective-permute-start.21 = (f32[48,1152]{1,0:T(8,128)S(1)}, f32[48,1152]{1,0:T(8,128)S(1)}, u32[]{:S(2)}, u32[]{:S(2)}) collective-permute-start(f32[48,1152]{1,0:T(8,128)S(1)} %get-tuple-element.56), channel_id=1, source_target_pairs={{0,24},{4,28},{8,16},{12,20},{16,8},{20,12},{24,0},{28,4},{1,25},{... | collective-permute-start | bytes 663560 | tf_op jit(solution)/shard_map/ppermute | solution.py:405
  96.4 2.0 %collective-permute-start.27 = (f32[48,1152]{1,0:T(8,128)S(1)}, f32[48,1152]{1,0:T(8,128)S(1)}, u32[]{:S(2)}, u32[]{:S(2)}) collective-permute-start(f32[48,1152]{1,0:T(8,128)S(1)} %get-tuple-element.66), channel_id=1, source_target_pairs={{0,8},{4,12},{8,0},{12,4},{16,24},{20,28},{24,16},{28,20},{1,9},{5... | collective-permute-start | bytes 663560 | tf_op jit(solution)/shard_map/ppermute | solution.py:405
  98.4 1.4 %collective-permute-done.19.refs_5_ = f32[48,1152]{1,0:T(8,128)S(1)} collective-permute-done((f32[48,1152]{1,0:T(8,128)S(1)}, f32[48,1152]{1,0:T(8,128)S(1)}, u32[]{:S(2)}, u32[]{:S(2)}) %collective-permute-start.19) | collective-permute-done | bytes 221216 | tf_op jit(solution)/shard_map/ppermute | solution.py:405
  100.3 6.3 %collective-permute-done.20.refs_6_ = f32[48,1152]{1,0:T(8,128)S(1)} collective-permute-done((f32[48,1152]{1,0:T(8,128)S(1)}, f32[48,1152]{1,0:T(8,128)S(1)}, u32[]{:S(2)}, u32[]{:S(2)}) %collective-permute-start.20) | collective-permute-done | bytes 221216 | tf_op jit(solution)/shard_map/ppermute | solution.py:405
  106.6 2.8 %collective-permute-done.27.refs_9_ = f32[48,1152]{1,0:T(8,128)S(1)} collective-permute-done((f32[48,1152]{1,0:T(8,128)S(1)}, f32[48,1152]{1,0:T(8,128)S(1)}, u32[]{:S(2)}, u32[]{:S(2)}) %collective-permute-start.27) | collective-permute-done | bytes 221216 | tf_op jit(solution)/shard_map/ppermute | solution.py:405
  109.4 6.0 %collective-permute-done.28.refs_10_ = f32[48,1152]{1,0:T(8,128)S(1)} collective-permute-done((f32[48,1152]{1,0:T(8,128)S(1)}, f32[48,1152]{1,0:T(8,128)S(1)}, u32[]{:S(2)}, u32[]{:S(2)}) %collective-permute-start.28) | collective-permute-done | bytes 221216 | tf_op jit(solution)/shard_map/ppermute | solution.py:405
  115.3 2.1 %place.1 = f32[576,1152]{1,0:T(8,128)} custom-call(f32[48,1152]{1,0:T(8,128)S(1)} %get-tuple-element.41.refs_0_, f32[48,1152]{1,0:T(8,128)S(1)} %collective-permute-done.8.refs_1_, f32[48,1152]{1,0:T(8,128)S(1)} %collective-permute-done.9.refs_2_, f32[48,1152]{1,0:T(8,128)S(1)} %collective-permute-done.10.refs_3_, f32[48,1152]{1,0:T(8,128)S(1)} %get-tuple-element.53.refs_4_, ...), custom_call_target="tpu_custom_call" | custom-call | tf_op jit(solution)/shard_map/place/pallas_call | solution.py:357
  (80 shorter events, 24.0 us)
Async XLA Ops:
  11.5 17.7 %collective-permute-start.1 = (f32[64,1536]{1,0:T(8,128)}, f32[64,1536]{1,0:T(8,128)S(1)}, u32[]{:S(2)}, u32[]{:S(2)}) collective-permute-start(f32[64,1536]{1,0:T(8,128)} %get-tuple-element.37.own), channel_id=1, source_target_pairs={{0,1},{3,2},{4,5},{7,6},{8,9},{11,10},{12,13},{15,14},{16,17},{19,... | collective-permute-start | bytes 1179656 | tf_op jit(solution)/shard_map/ppermute | solution.py:408
  16.5 13.6 %collective-permute-start = (f32[64,1536]{1,0:T(8,128)}, f32[64,1536]{1,0:T(8,128)S(1)}, u32[]{:S(2)}, u32[]{:S(2)}) collective-permute-start(f32[64,1536]{1,0:T(8,128)} %get-tuple-element.37.own), channel_id=1, source_target_pairs={{1,2},{2,1},{5,6},{6,5},{9,10},{10,9},{13,14},{14,13},{17,18},{18,... | collective-permute-start | bytes 1179656 | tf_op jit(solution)/shard_map/ppermute | solution.py:408
  18.7 10.5 %collective-permute-start.12 = (f32[128,384]{1,0:T(8,128)}, f32[128,384]{1,0:T(8,128)S(1)}, u32[]{:S(2)}, u32[]{:S(2)}) collective-permute-start(f32[128,384]{1,0:T(8,128)} %get-tuple-element.47), channel_id=1, source_target_pairs={{0,16},{4,20},{8,24},{12,28},{16,0},{20,4},{24,8},{28,12},{1,17},{... | collective-permute-start | bytes 589832 | tf_op jit(solution)/shard_map/ppermute | solution.py:405
  20.2 9.7 %collective-permute-start.13 = (f32[128,384]{1,0:T(8,128)}, f32[128,384]{1,0:T(8,128)S(1)}, u32[]{:S(2)}, u32[]{:S(2)}) collective-permute-start(f32[128,384]{1,0:T(8,128)} %get-tuple-element.48), channel_id=1, source_target_pairs={{0,24},{4,28},{8,16},{12,20},{16,8},{20,12},{24,0},{28,4},{1,25},{... | collective-permute-start | bytes 589832 | tf_op jit(solution)/shard_map/ppermute | solution.py:405
  30.0 11.0 %collective-permute-start.15 = (f32[64,1536]{1,0:T(8,128)S(1)}, f32[64,1536]{1,0:T(8,128)S(1)}, u32[]{:S(2)}, u32[]{:S(2)}) collective-permute-start(f32[64,1536]{1,0:T(8,128)S(1)} %pad_maximum_fusion.1.own), channel_id=1, source_target_pairs={{0,1},{3,2},{4,5},{7,6},{8,9},{11,10},{12,13},{15,14},{16,17},{19,... | collective-permute-start | bytes 1179656 | tf_op jit(solution)/shard_map/ppermute | solution.py:408
  37.4 14.5 %collective-permute-start.3 = (f32[96,1536]{1,0:T(8,128)S(1)}, f32[96,1536]{1,0:T(8,128)S(1)}, u32[]{:S(2)}, u32[]{:S(2)}) collective-permute-start(f32[96,1536]{1,0:T(8,128)S(1)} %get-tuple-element.40), channel_id=1, source_target_pairs={{1,0},{2,3},{5,4},{6,7},{9,8},{10,11},{13,12},{14,15},{17,16},{18,... | collective-permute-start | bytes 1769480 | tf_op jit(solution)/shard_map/ppermute | solution.py:408
  38.7 16.4 %collective-permute-start.14 = (f32[64,1536]{1,0:T(8,128)S(1)}, f32[64,1536]{1,0:T(8,128)S(1)}, u32[]{:S(2)}, u32[]{:S(2)}) collective-permute-start(f32[64,1536]{1,0:T(8,128)S(1)} %pad_maximum_fusion.1.own), channel_id=1, source_target_pairs={{1,2},{2,1},{5,6},{6,5},{9,10},{10,9},{13,14},{14,13},{17,18},{18,... | collective-permute-start | bytes 1179656 | tf_op jit(solution)/shard_map/ppermute | solution.py:408
  41.0 15.1 %collective-permute-start.16 = (f32[64,1536]{1,0:T(8,128)S(1)}, f32[64,1536]{1,0:T(8,128)S(1)}, u32[]{:S(2)}, u32[]{:S(2)}) collective-permute-start(f32[64,1536]{1,0:T(8,128)S(1)} %collective-permute-done.15.outer), channel_id=1, source_target_pairs={{1,2},{2,1},{5,6},{6,5},{9,10},{10,9},{13,14},{14,13},{17,18},{18,... | collective-permute-start | bytes 1179656 | tf_op jit(solution)/shard_map/ppermute | solution.py:408
  41.8 16.4 %collective-permute-start.23 = (f32[64,1536]{1,0:T(8,128)S(1)}, f32[64,1536]{1,0:T(8,128)S(1)}, u32[]{:S(2)}, u32[]{:S(2)}) collective-permute-start(f32[64,1536]{1,0:T(8,128)S(1)} %pad_maximum_fusion.2.own), channel_id=1, source_target_pairs={{0,1},{3,2},{4,5},{7,6},{8,9},{11,10},{12,13},{15,14},{16,17},{19,... | collective-permute-start | bytes 1179656 | tf_op jit(solution)/shard_map/ppermute | solution.py:408
  56.8 12.2 %collective-permute-start.17 = (f32[96,1536]{1,0:T(8,128)S(1)}, f32[96,1536]{1,0:T(8,128)S(1)}, u32[]{:S(2)}, u32[]{:S(2)}) collective-permute-start(f32[96,1536]{1,0:T(8,128)S(1)} %get-tuple-element.52), channel_id=1, source_target_pairs={{1,0},{2,3},{5,4},{6,7},{9,8},{10,11},{13,12},{14,15},{17,16},{18,... | collective-permute-start | bytes 1769480 | tf_op jit(solution)/shard_map/ppermute | solution.py:408
  58.1 11.0 %collective-permute-start.22 = (f32[64,1536]{1,0:T(8,128)S(1)}, f32[64,1536]{1,0:T(8,128)S(1)}, u32[]{:S(2)}, u32[]{:S(2)}) collective-permute-start(f32[64,1536]{1,0:T(8,128)S(1)} %pad_maximum_fusion.2.own), channel_id=1, source_target_pairs={{1,2},{2,1},{5,6},{6,5},{9,10},{10,9},{13,14},{14,13},{17,18},{18,... | collective-permute-start | bytes 1179656 | tf_op jit(solution)/shard_map/ppermute | solution.py:408
  58.8 10.3 %collective-permute-start.24 = (f32[64,1536]{1,0:T(8,128)S(1)}, f32[64,1536]{1,0:T(8,128)S(1)}, u32[]{:S(2)}, u32[]{:S(2)}) collective-permute-start(f32[64,1536]{1,0:T(8,128)S(1)} %collective-permute-done.23.outer), channel_id=1, source_target_pairs={{1,2},{2,1},{5,6},{6,5},{9,10},{10,9},{13,14},{14,13},{17,18},{18,... | collective-permute-start | bytes 1179656 | tf_op jit(solution)/shard_map/ppermute | solution.py:408
  62.2 9.9 %collective-permute-start.7 = (f32[96,1536]{1,0:T(8,128)S(1)}, f32[96,1536]{1,0:T(8,128)S(1)}, u32[]{:S(2)}, u32[]{:S(2)}) collective-permute-start(f32[96,1536]{1,0:T(8,128)S(1)} %pad_maximum_fusion.mine), channel_id=1, source_target_pairs={{0,4},{4,0},{8,12},{12,8},{16,20},{20,16},{24,28},{28,24},{1,5},{5... | collective-permute-start | bytes 1769480 | tf_op jit(solution)/shard_map/ppermute | solution.py:405
  69.8 17.8 %collective-permute-start.25 = (f32[96,1536]{1,0:T(8,128)S(1)}, f32[96,1536]{1,0:T(8,128)S(1)}, u32[]{:S(2)}, u32[]{:S(2)}) collective-permute-start(f32[96,1536]{1,0:T(8,128)S(1)} %get-tuple-element.63), channel_id=1, source_target_pairs={{1,0},{2,3},{5,4},{6,7},{9,8},{10,11},{13,12},{14,15},{17,16},{18,... | collective-permute-start | bytes 1769480 | tf_op jit(solution)/shard_map/ppermute | solution.py:408
  73.5 14.2 %collective-permute-start.10 = (f32[48,1152]{1,0:T(8,128)S(1)}, f32[48,1152]{1,0:T(8,128)S(1)}, u32[]{:S(2)}, u32[]{:S(2)}) collective-permute-start(f32[48,1152]{1,0:T(8,128)S(1)} %get-tuple-element.44), channel_id=1, source_target_pairs={{0,24},{4,28},{8,16},{12,20},{16,8},{20,12},{24,0},{28,4},{1,25},{... | collective-permute-start | bytes 663560 | tf_op jit(solution)/shard_map/ppermute | solution.py:405
  76.6 11.1 %collective-permute-start.8 = (f32[48,1152]{1,0:T(8,128)S(1)}, f32[48,1152]{1,0:T(8,128)S(1)}, u32[]{:S(2)}, u32[]{:S(2)}) collective-permute-start(f32[48,1152]{1,0:T(8,128)S(1)} %get-tuple-element.42), channel_id=1, source_target_pairs={{0,8},{4,12},{8,0},{12,4},{16,24},{20,28},{24,16},{28,20},{1,9},{5... | collective-permute-start | bytes 663560 | tf_op jit(solution)/shard_map/ppermute | solution.py:405
  77.9 9.8 %collective-permute-start.9 = (f32[48,1152]{1,0:T(8,128)S(1)}, f32[48,1152]{1,0:T(8,128)S(1)}, u32[]{:S(2)}, u32[]{:S(2)}) collective-permute-start(f32[48,1152]{1,0:T(8,128)S(1)} %get-tuple-element.43), channel_id=1, source_target_pairs={{0,16},{4,20},{8,24},{12,28},{16,0},{20,4},{24,8},{28,12},{1,17},{... | collective-permute-start | bytes 663560 | tf_op jit(solution)/shard_map/ppermute | solution.py:405
  79.3 8.5 %collective-permute-start.18 = (f32[96,1536]{1,0:T(8,128)S(1)}, f32[96,1536]{1,0:T(8,128)S(1)}, u32[]{:S(2)}, u32[]{:S(2)}) collective-permute-start(f32[96,1536]{1,0:T(8,128)S(1)} %add.185.mine), channel_id=1, source_target_pairs={{0,4},{4,0},{8,12},{12,8},{16,20},{20,16},{24,28},{28,24},{1,5},{5... | collective-permute-start | bytes 1769480 | tf_op jit(solution)/shard_map/ppermute | solution.py:405
  89.1 10.7 %collective-permute-start.19 = (f32[48,1152]{1,0:T(8,128)S(1)}, f32[48,1152]{1,0:T(8,128)S(1)}, u32[]{:S(2)}, u32[]{:S(2)}) collective-permute-start(f32[48,1152]{1,0:T(8,128)S(1)} %get-tuple-element.54), channel_id=1, source_target_pairs={{0,8},{4,12},{8,0},{12,4},{16,24},{20,28},{24,16},{28,20},{1,9},{5... | collective-permute-start | bytes 663560 | tf_op jit(solution)/shard_map/ppermute | solution.py:405
  93.6 13.0 %collective-permute-start.20 = (f32[48,1152]{1,0:T(8,128)S(1)}, f32[48,1152]{1,0:T(8,128)S(1)}, u32[]{:S(2)}, u32[]{:S(2)}) collective-permute-start(f32[48,1152]{1,0:T(8,128)S(1)} %get-tuple-element.55), channel_id=1, source_target_pairs={{0,16},{4,20},{8,24},{12,28},{16,0},{20,4},{24,8},{28,12},{1,17},{... | collective-permute-start | bytes 663560 | tf_op jit(solution)/shard_map/ppermute | solution.py:405
  93.6 13.0 %collective-permute-start.21 = (f32[48,1152]{1,0:T(8,128)S(1)}, f32[48,1152]{1,0:T(8,128)S(1)}, u32[]{:S(2)}, u32[]{:S(2)}) collective-permute-start(f32[48,1152]{1,0:T(8,128)S(1)} %get-tuple-element.56), channel_id=1, source_target_pairs={{0,24},{4,28},{8,16},{12,20},{16,8},{20,12},{24,0},{28,4},{1,25},{... | collective-permute-start | bytes 663560 | tf_op jit(solution)/shard_map/ppermute | solution.py:405
  96.4 13.0 %collective-permute-start.27 = (f32[48,1152]{1,0:T(8,128)S(1)}, f32[48,1152]{1,0:T(8,128)S(1)}, u32[]{:S(2)}, u32[]{:S(2)}) collective-permute-start(f32[48,1152]{1,0:T(8,128)S(1)} %get-tuple-element.66), channel_id=1, source_target_pairs={{0,8},{4,12},{8,0},{12,4},{16,24},{20,28},{24,16},{28,20},{1,9},{5... | collective-permute-start | bytes 663560 | tf_op jit(solution)/shard_map/ppermute | solution.py:405
  98.4 16.9 %collective-permute-start.28 = (f32[48,1152]{1,0:T(8,128)S(1)}, f32[48,1152]{1,0:T(8,128)S(1)}, u32[]{:S(2)}, u32[]{:S(2)}) collective-permute-start(f32[48,1152]{1,0:T(8,128)S(1)} %get-tuple-element.67), channel_id=1, source_target_pairs={{0,16},{4,20},{8,24},{12,28},{16,0},{20,4},{24,8},{28,12},{1,17},{... | collective-permute-start | bytes 663560 | tf_op jit(solution)/shard_map/ppermute | solution.py:405
  99.9 15.5 %collective-permute-start.29 = (f32[48,1152]{1,0:T(8,128)S(1)}, f32[48,1152]{1,0:T(8,128)S(1)}, u32[]{:S(2)}, u32[]{:S(2)}) collective-permute-start(f32[48,1152]{1,0:T(8,128)S(1)} %get-tuple-element.68), channel_id=1, source_target_pairs={{0,24},{4,28},{8,16},{12,20},{16,8},{20,12},{24,0},{28,4},{1,25},{... | collective-permute-start | bytes 663560 | tf_op jit(solution)/shard_map/ppermute | solution.py:405
  (7 other events, 40.7 us)
